TPU v7x, 512 devices: a whole 4x8x8 slice. The times are simulated.
512 devices in a mesh: ep: 16 (over y, core), etp: 32 (over z, x).
Axes of the slice: x: 4, y: 8, z: 8, core: 2. Of those that a mesh axis runs over, the one named last changes fastest.
Arguments:
- tokens: bfloat16 [2048, 3072], P('ep', 'etp'), may hold values from -6 to 6
- routes: int32 [2048, 4], P('ep'), may hold values from 0 to 15, all different within a row; in each aligned block of 128 rows (0 to 127, 128 to 255, ...) at most 36 rows name the same one
- gate_fixed: int32 [2048, 4], P('ep'), may hold values from 3277 to 65535
- gate_weight: bfloat16 [16, 8192, 3072], P('ep', 'etp'), may hold values from -0.21875 to 0.21875
- up_weight: bfloat16 [16, 8192, 3072], P('ep', 'etp'), may hold values from -0.21875 to 0.21875
- down_weight: bfloat16 [16, 8192, 3072], P('ep', 'etp'), may hold values from -0.125 to 0.125
- cotangent: bfloat16 [2048, 3072], P('ep', 'etp'), may hold values from -6 to 6
Outputs:
- layer_output: bfloat16 [2048, 3072], P('ep', 'etp')
- grad_tokens: bfloat16 [2048, 3072], P('ep', 'etp')
Inputs may be any that keep to these rules, and one draw needn't show every extreme that they name: `routes`: A row names 4 different experts. Among the 128 rows of one ep index no expert is named by more than 36 rows, and in every draw some expert is named by exactly 36 rows of some ep index.
All inputs are finite; a program needn't handle non-finite values.
Results may differ from a plain program's by a relative error of at most 0.02.
Values may be sent and summed in bfloat16 or wider, within the bound.
No kernel may reach another device: no remote copies, remote signals or barrier semaphores. Data moves between devices by JAX's collectives and lax.ppermute only.
A program may use at most 128 MiB of HBM per device.

v0:
```python
import jax
import jax.numpy as jnp
from jax import lax
from jax.sharding import PartitionSpec as P

fixed_point = 65536.0


def silu_parts(pre_gate):
    sigmoid_value = jax.nn.sigmoid(pre_gate)
    activated = pre_gate * sigmoid_value
    derivative = sigmoid_value * (1.0 + pre_gate * (1.0 - sigmoid_value))
    return (activated, derivative)


def slot_layout(routes, capacity, experts):
    token_count, fanout = routes.shape
    entries = token_count * fanout
    flattened = routes.reshape(entries)
    onehot = (flattened[:, None] == jnp.arange(experts, dtype=jnp.int32)[None, :]).astype(jnp.int32)
    earlier = jnp.cumsum(onehot, axis=0) - onehot
    target = flattened * capacity + jnp.sum(earlier * onehot, axis=1)
    slot_table = (
        jnp.full((experts * capacity,), entries, jnp.int32)
        .at[target]
        .set(jnp.arange(entries, dtype=jnp.int32))
    )
    return (target, slot_table)


def arrange_rows(values, slot_table, fanout, experts):
    padded = jnp.concatenate([values, jnp.zeros((1, values.shape[1]), values.dtype)], axis=0)
    chosen = jnp.take(padded, slot_table // fanout, axis=0)
    return chosen.reshape(experts, -1, values.shape[1])


def arrange_scaled(values, scales, slot_table, fanout, experts):
    padded = jnp.concatenate([values, jnp.zeros((1, values.shape[1]), values.dtype)], axis=0)
    scale_pad = jnp.concatenate([scales, jnp.zeros((1,), jnp.float32)])
    chosen = jnp.take(padded, slot_table // fanout, axis=0).astype(jnp.float32)
    scaled = (chosen * jnp.take(scale_pad, slot_table)[:, None]).astype(jnp.bfloat16)
    return scaled.reshape(experts, -1, values.shape[1])


def shards(tokens, routes, gate_fixed, gate_weight, up_weight, down_weight, cotangent):
    experts = lax.axis_size("ep")
    token_count, fanout = routes.shape
    capacity = min(token_count, token_count * fanout * 9 // (8 * experts))
    target, slot_table = slot_layout(routes, capacity, experts)
    gate_value = gate_fixed.astype(jnp.float32) / fixed_point
    gate_flat = gate_value.reshape(token_count * fanout)
    gate_matrix = gate_weight[0]
    up_matrix = up_weight[0]
    down_matrix = down_weight[0]
    features = lax.all_gather(tokens, "etp", axis=1, tiled=True)
    outgoing = arrange_rows(features, slot_table, fanout, experts)
    received = lax.all_to_all(outgoing, "ep", split_axis=0, concat_axis=0, tiled=True)
    cot_full = lax.all_gather(cotangent, "etp", axis=1, tiled=True)
    grad_send = arrange_scaled(cot_full, gate_flat, slot_table, fanout, experts)
    grad_in = lax.all_to_all(grad_send, "ep", split_axis=0, concat_axis=0, tiled=True)
    row_total = experts * capacity
    contract = (((1,), (1,)), ((), ()))
    flat_rows = received.reshape(row_total, -1)
    pre_gate = lax.dot_general(flat_rows, gate_matrix, contract, preferred_element_type=jnp.float32)
    pre_up = lax.dot_general(flat_rows, up_matrix, contract, preferred_element_type=jnp.float32)
    activated, derivative = silu_parts(pre_gate)
    hidden = (activated * pre_up).astype(jnp.bfloat16)
    partial_value = jnp.dot(hidden, down_matrix, preferred_element_type=jnp.float32).astype(
        jnp.bfloat16
    )
    returned = lax.all_to_all(
        partial_value.reshape(experts, capacity, -1), "ep", split_axis=0, concat_axis=0, tiled=True
    )
    picked = jnp.take(returned.reshape(row_total, -1), target, axis=0).reshape(
        token_count, fanout, -1
    )
    mixed_part = jnp.sum(picked.astype(jnp.float32) * gate_value[:, :, None], axis=1).astype(
        jnp.bfloat16
    )
    layer_output = lax.psum_scatter(
        mixed_part.astype(jnp.float32).astype(jnp.bfloat16), "etp", scatter_dimension=1, tiled=True
    )
    grad_rows = grad_in.reshape(row_total, -1)
    grad_hidden = lax.dot_general(
        grad_rows, down_matrix, contract, preferred_element_type=jnp.float32
    )
    grad_gate = (grad_hidden * pre_up * derivative).astype(jnp.bfloat16)
    grad_up = (grad_hidden * activated).astype(jnp.bfloat16)
    part_in = jnp.dot(grad_gate, gate_matrix, preferred_element_type=jnp.float32)
    part_in = (part_in + jnp.dot(grad_up, up_matrix, preferred_element_type=jnp.float32)).astype(
        jnp.bfloat16
    )
    gradient_back = lax.all_to_all(
        part_in.reshape(experts, capacity, -1), "ep", split_axis=0, concat_axis=0, tiled=True
    )
    picked_grads = jnp.take(gradient_back.reshape(row_total, -1), target, axis=0).reshape(
        token_count, fanout, -1
    )
    grad_part = jnp.sum(picked_grads.astype(jnp.float32), axis=1).astype(jnp.bfloat16)
    grad_tokens = lax.psum_scatter(
        grad_part.astype(jnp.float32).astype(jnp.bfloat16), "etp", scatter_dimension=1, tiled=True
    )
    return (layer_output, grad_tokens)


def solution(mesh):
    placed = (
        P("ep", "etp"),
        P("ep", None),
        P("ep", None),
        P("ep", "etp", None),
        P("ep", "etp", None),
        P("ep", "etp", None),
        P("ep", "etp"),
    )
    return jax.shard_map(
        shards,
        mesh=mesh,
        in_specs=placed,
        out_specs=(P("ep", "etp"), P("ep", "etp")),
        check_vma=False,
    )
```

profile of v0, /device:TPU:1, one launch (start us, length us, event | category | flops | bytes accessed | tf_op | source)
XLA Modules:
  0.0 925.9 jit_solution(17688045346712388084)
XLA Ops:
  7.2 0.8 broadcast_multiply_fusion
  8.0 0.8 copy.30
  9.2 1.2 reduce-window.6
  10.8 2.4 scatter_custom_fusion
  13.2 44.5 %all_gather.6 = bf16[128,3072]{0,1:T(8,128)(2,1)S(1)} all-gather(bf16[128,96]{0,1:T(8,128)(2,1)} %param.11), channel_id=1, replica_groups=mesh['ep'=16,'etp'=32] {'etp'}, dimensions={1}, use_global_device_ids=true | all-gather | bytes 811008 | tf_op jit(solution)/shard_map/all_gather | solution.py:55
  57.8 0.3 copy.34
  58.1 4.6 gather_fusion.1
  62.7 4.2 broadcast_select_fusion
  66.9 4.7 reshape.102
  71.6 20.2 %all-to-all-start = ((bf16[16,36,3072]{2,1,0:T(8,128)(2,1)}), bf16[16,36,3072]{2,1,0:T(8,128)(2,1)}, u32[]{:S(2)}, u32[]{:S(2)}) async-start(bf16[16,36,3072]{2,1,0:T(8,128)(2,1)} %reshape.102), calls=%async_computation | async-start | bytes 7864320 | tf_op jit(solution)/shard_map/all_to_all | solution.py:57
  91.9 0.6 copy-done.7
  92.6 41.9 %all_gather.7 = bf16[128,3072]{0,1:T(8,128)(2,1)S(1)} all-gather(bf16[128,96]{0,1:T(8,128)(2,1)S(1)} %copy-done.9), channel_id=1, replica_groups=mesh['ep'=16,'etp'=32] {'etp'}, dimensions={1}, use_global_device_ids=true | all-gather | bytes 811008 | tf_op jit(solution)/shard_map/all_gather | solution.py:58
  134.5 0.3 copy.36
  134.9 4.7 gather_fusion.3
  139.6 2.6 gather_fusion
  142.2 5.9 multiply_convert_fusion
  148.1 4.7 reshape.107
  152.8 26.9 %all-to-all-done = bf16[16,36,3072]{2,1,0:T(8,128)(2,1)} async-done(((bf16[16,36,3072]{2,1,0:T(8,128)(2,1)}), bf16[16,36,3072]{2,1,0:T(8,128)(2,1)}, u32[]{:S(2)}, u32[]{:S(2)}) %all-to-all-start) | async-done | bytes 3538976 | tf_op jit(solution)/shard_map/all_to_all | solution.py:57
  179.7 5.5 all-to-all-start.2
  185.3 4.7 reshape.103
  189.9 3.7 fusion.8
  193.9 1.1 fusion.4
  195.1 3.0 convolution_convert_fusion
  198.0 4.8 reshape.104
  202.8 70.4 %all-to-all-done.2 = bf16[16,36,3072]{2,1,0:T(8,128)(2,1)} async-done(((bf16[16,36,3072]{2,1,0:T(8,128)(2,1)}), bf16[16,36,3072]{2,1,0:T(8,128)(2,1)}, u32[]{:S(2)}, u32[]{:S(2)}) %all-to-all-start.2) | async-done | bytes 3538976 | tf_op jit(solution)/shard_map/all_to_all | solution.py:60
  273.2 5.5 all-to-all-start.1
  278.8 4.7 reshape.108
  283.5 3.2 fusion
  286.7 1.2 fusion.6
  288.1 2.2 add_convert_fusion
  290.4 2.6 reshape.109
  293.0 73.8 %all-to-all-done.1 = bf16[16,36,3072]{2,1,0:T(8,128)(2,1)} async-done(((bf16[16,36,3072]{2,1,0:T(8,128)(2,1)}), bf16[16,36,3072]{2,1,0:T(8,128)(2,1)}, u32[]{:S(2)}, u32[]{:S(2)}) %all-to-all-start.1) | async-done | bytes 3538976 | tf_op jit(solution)/shard_map/all_to_all | solution.py:71
  366.8 5.5 all-to-all-start.3
  372.6 3.1 reshape.105
  375.7 3.8 gather_fusion.2
  379.6 80.7 %all-to-all-done.3 = bf16[16,36,3072]{2,1,0:T(8,128)(2,1)} async-done(((bf16[16,36,3072]{2,1,0:T(8,128)(2,1)}), bf16[16,36,3072]{2,1,0:T(8,128)(2,1)}, u32[]{:S(2)}, u32[]{:S(2)}) %all-to-all-start.3) | async-done | bytes 3538976 | tf_op jit(solution)/shard_map/all_to_all | solution.py:93
  460.3 3.1 reshape.110
  463.4 3.9 gather_fusion.4
  467.3 7.1 broadcast_select_fusion.1
  474.5 4.8 reshape.111
  479.3 5.2 reduce_sum.35
  484.5 2.3 copy.42
  486.8 0.3 reduce-scatter.7.cloned.1.call-start
  487.2 7.7 reshape.112
  494.9 7.6 multiply_reduce_fusion
  502.5 1.2 copy.40
  503.7 192.6 %reduce-scatter.9.cloned.1.call-done = bf16[96,128]{1,0:T(8,128)(2,1)} async-done(((bf16[3072,128]{1,0:T(8,128)(2,1)}), bf16[96,128]{1,0:T(8,128)(2,1)}) %reduce-scatter.9.cloned.1.call-update) | async-done | bytes 24592
  696.3 222.8 %reduce-scatter.7.cloned.1.call-done = bf16[96,128]{1,0:T(8,128)(2,1)} async-done(((bf16[3072,128]{1,0:T(8,128)(2,1)}), bf16[96,128]{1,0:T(8,128)(2,1)}) %reduce-scatter.7.cloned.1.call-update) | async-done | bytes 24592
  (48 shorter events, 2.0 us)
Async XLA Ops:
  7.2 187.9 %copy-start = (bf16[1,256,3072]{2,1,0:T(8,128)(2,1)S(1)}, bf16[1,256,3072]{2,1,0:T(8,128)(2,1)}, u32[]{:S(2)}) copy-start(bf16[1,256,3072]{2,1,0:T(8,128)(2,1)} %param.16) | copy-start | bytes 4718596
  71.6 20.2 %copy-start.10 = (s32[128,4]{0,1:T(4,128)S(1)}, s32[128,4]{0,1:T(4,128)}, u32[]{:S(2)}) copy-start(s32[128,4]{0,1:T(4,128)} %param.13) | copy-start | bytes 6148
  71.6 21.0 %copy-start.9 = (bf16[128,96]{0,1:T(8,128)(2,1)S(1)}, bf16[128,96]{0,1:T(8,128)(2,1)}, u32[]{:S(2)}) copy-start(bf16[128,96]{0,1:T(8,128)(2,1)} %param.17) | copy-start | bytes 73732
  71.6 108.2 %all-to-all-start = ((bf16[16,36,3072]{2,1,0:T(8,128)(2,1)}), bf16[16,36,3072]{2,1,0:T(8,128)(2,1)}, u32[]{:S(2)}, u32[]{:S(2)}) async-start(bf16[16,36,3072]{2,1,0:T(8,128)(2,1)} %reshape.102), calls=%async_computation | async-start | bytes 7864320 | tf_op jit(solution)/shard_map/all_to_all | solution.py:57
  91.9 0.6 copy-start.7
  179.7 93.5 %all-to-all-start.2 = ((bf16[16,36,3072]{2,1,0:T(8,128)(2,1)}), bf16[16,36,3072]{2,1,0:T(8,128)(2,1)}, u32[]{:S(2)}, u32[]{:S(2)}) async-start(bf16[16,36,3072]{2,1,0:T(8,128)(2,1)} %reshape.107), calls=%async_computation.2 | async-start | bytes 7864320 | tf_op jit(solution)/shard_map/all_to_all | solution.py:60
  189.9 3.8 copy-start.3
  189.9 4.0 copy-start.5
  193.9 92.8 %copy-start.2 = (f32[576,256]{1,0:T(8,128)}, f32[576,256]{1,0:T(8,128)S(1)}, u32[]{:S(2)}) copy-start(f32[576,256]{1,0:T(8,128)S(1)} %fusion.8) | copy-start | bytes 1769476
  273.2 93.5 %all-to-all-start.1 = ((bf16[16,36,3072]{2,1,0:T(8,128)(2,1)}), bf16[16,36,3072]{2,1,0:T(8,128)(2,1)}, u32[]{:S(2)}, u32[]{:S(2)}) async-start(bf16[16,36,3072]{2,1,0:T(8,128)(2,1)} %reshape.104), calls=%async_computation.1 | async-start | bytes 7864320 | tf_op jit(solution)/shard_map/all_to_all | solution.py:71
  283.5 3.3 copy-start.4
  286.7 1.4 copy-start.6
  366.8 93.5 %all-to-all-start.3 = ((bf16[16,36,3072]{2,1,0:T(8,128)(2,1)}), bf16[16,36,3072]{2,1,0:T(8,128)(2,1)}, u32[]{:S(2)}, u32[]{:S(2)}) async-start(bf16[16,36,3072]{2,1,0:T(8,128)(2,1)} %reshape.109), calls=%async_computation.3 | async-start | bytes 7864320 | tf_op jit(solution)/shard_map/all_to_all | solution.py:93
  372.3 324.0 %reduce-scatter.9.cloned.1.call-start = ((), (), s32[]{:S(2)}) async-start(), calls=%async_computation.7 | async-start | bytes 811008
  486.8 432.3 %reduce-scatter.7.cloned.1.call-start = ((), (), s32[]{:S(2)}) async-start(), calls=%async_computation.6 | async-start | bytes 811008
  487.1 7.7 copy-start.8
  487.1 431.9 %copy-start.1 = (bf16[1,256,3072]{2,1,0:T(8,128)(2,1)S(1)}, bf16[1,256,3072]{2,1,0:T(8,128)(2,1)}, u32[]{:S(2)}) copy-start(bf16[1,256,3072]{2,1,0:T(8,128)(2,1)} %param.16) | copy-start | bytes 4718596
Sparse Core Ops, SparseCore 0:
  486.9 209.3 reduce-scatter.8
  701.3 217.7 reduce-scatter.6
where the time goes:
time: 932 us; the launch traced here: 926 us
  waiting for transfers between devices  667 us (72%)
  blocking collectives  86.4 us (9%)
  local copies, waits for them, and re-layouts  73.8 us (8%)
  starting transfers between devices  37.4 us (4%)
  other arithmetic  32.2 us (3%)
  matrix products  14.5 us (2%)
  between operations  14.3 us (2%)
    unnamed x4, waiting for transfers between devices  415 us
    all_to_all x1, waiting for transfers between devices, shards(): lax.all_to_all(part_in.reshape(experts, capacity, -1), 'ep', split_axis=0...  80.7 us
    all_to_all x1, waiting for transfers between devices, shards(): lax.all_to_all(partial_value.reshape(experts, capacity, -1), 'ep', split_...  73.8 us
    all_to_all x1, waiting for transfers between devices, shards(): lax.all_to_all(grad_send, 'ep', split_axis=0, concat_axis=0, tiled=True)  70.4 us
    all_gather x1, blocking collectives, shards(): features = lax.all_gather(tokens, 'etp', axis=1, tiled=True)  44.5 us
    all_gather x1, blocking collectives, shards(): cot_full = lax.all_gather(cotangent, 'etp', axis=1, tiled=True)  41.9 us
    all_to_all x1, waiting for transfers between devices, shards(): lax.all_to_all(outgoing, 'ep', split_axis=0, concat_axis=0, tiled=True)  26.9 us
    all_to_all x1, starting transfers between devices, shards(): lax.all_to_all(outgoing, 'ep', split_axis=0, concat_axis=0, tiled=True)  20.2 us
  transfers between devices with their start and end apart: 6, of which 6 were waited for; matrix products, arithmetic and copies ran while one was open for 8% of the time, Pallas kernels for 0%

commit v1 on v0

v1 whole, which is shorter than its diff:
```python
import functools

import jax
import jax.numpy as jnp
from jax import lax
from jax.experimental import pallas as pl
from jax.experimental.pallas import tpu as pltpu
from jax.sharding import Mesh
from jax.sharding import PartitionSpec as P

EXPERTS = 16
CAP = 36
TOKENS_HERE = 128
FEATURES = 96
ROWS = EXPERTS * CAP
BOTH = 2 * ROWS
HIDDEN = 256
MAIN = 512
TAIL = ROWS - MAIN
EP = ("y", "c")
NT = (((1,), (1,)), ((), ()))
TN = (((0,), (0,)), ((), ()))


def f32_dot(a, b, dims):
    return lax.dot_general(a, b, dims, preferred_element_type=jnp.float32)


def slots(routes, gate_fixed):
    named = []
    gates = []
    for e in range(EXPERTS):
        hit = routes == e
        named.append(jnp.sum(hit.astype(jnp.float32), axis=0, keepdims=True))
        gates.append(jnp.sum(jnp.where(hit, gate_fixed, 0).astype(jnp.float32), axis=0, keepdims=True))
    member = jnp.concatenate(named, axis=0)
    before = lax.broadcasted_iota(jnp.int32, (TOKENS_HERE, TOKENS_HERE), 0)
    after = lax.broadcasted_iota(jnp.int32, (TOKENS_HERE, TOKENS_HERE), 1)
    earlier = (before < after).astype(jnp.bfloat16)
    rank = jnp.dot(member.astype(jnp.bfloat16), earlier, preferred_element_type=jnp.float32)
    rank = jnp.where(member > 0.0, rank, -1.0)
    slot = lax.broadcasted_iota(jnp.int32, (2 * CAP, TOKENS_HERE), 0)
    slot = jnp.where(slot >= CAP, slot - CAP, slot).astype(jnp.float32)
    onehot = [(rank[e : e + 1] == slot).astype(jnp.float32) for e in range(EXPERTS)]
    return onehot, gates


def row_of_slot(shape, axis):
    index = lax.broadcasted_iota(jnp.int32, shape, axis)
    return index - (index // (2 * CAP)) * (2 * CAP)


def dispatch_body(routes_ref, gate_ref, tokens_ref, cot_ref, out_ref):
    onehot, gates = slots(routes_ref[...], gate_ref[...])
    scaled = [jnp.sum(onehot[e] * gates[e], axis=1, keepdims=True) for e in range(EXPERTS)]
    scale = jnp.concatenate(scaled, axis=0) * (1.0 / 65536.0)
    chosen = jnp.concatenate(onehot, axis=0).astype(jnp.bfloat16)
    from_tokens = f32_dot(chosen, tokens_ref[...], NT)
    from_cot = f32_dot(chosen, cot_ref[...], NT) * scale
    is_token = row_of_slot((BOTH, FEATURES), 0) < CAP
    out_ref[...] = jnp.where(is_token, from_tokens, from_cot).astype(jnp.bfloat16)


def column_of(row):
    source = row // (2 * CAP)
    within = row - source * (2 * CAP)
    is_cot = (within >= CAP).astype(jnp.int32)
    number = source * CAP + within - is_cot * CAP
    return jnp.where(number < MAIN, number + MAIN * is_cot, number + MAIN + TAIL * is_cot)


def placing():
    row = lax.broadcasted_iota(jnp.int32, (BOTH, 1), 0)
    column = lax.broadcasted_iota(jnp.int32, (BOTH, BOTH), 1)
    return (column_of(row) == column).astype(jnp.bfloat16)


def to_columns_body(rows_ref, out_ref):
    out_ref[...] = f32_dot(rows_ref[...], placing(), TN).astype(jnp.bfloat16)


def to_rows_body(columns_ref, out_ref):
    out_ref[...] = f32_dot(placing(), columns_ref[...], NT).astype(jnp.bfloat16)


def combine_body(routes_ref, gate_ref, rows_ref, out_ref, grad_ref):
    onehot, gates = slots(routes_ref[...], gate_ref[...])
    high, low = [], []
    for e in range(EXPERTS):
        top = jnp.floor(gates[e] * (1.0 / 256.0))
        high.append(onehot[e] * top)
        low.append(onehot[e] * (gates[e] - 256.0 * top))
    is_token = row_of_slot((BOTH, TOKENS_HERE), 0) < CAP
    high = jnp.where(is_token, jnp.concatenate(high, axis=0), 0.0).astype(jnp.bfloat16)
    low = jnp.where(is_token, jnp.concatenate(low, axis=0), 0.0).astype(jnp.bfloat16)
    whole = jnp.where(is_token, 0.0, jnp.concatenate(onehot, axis=0)).astype(jnp.bfloat16)
    rows = rows_ref[...]
    mixed = f32_dot(rows, high, TN) * (1.0 / 256.0) + f32_dot(rows, low, TN) * (1.0 / 65536.0)
    out_ref[...] = mixed.astype(jnp.bfloat16)
    grad_ref[...] = f32_dot(rows, whole, TN).astype(jnp.bfloat16)


def expert_body(x_ref, gate_ref, up_ref, down_ref, y_ref):
    gate, up, down = gate_ref[0], up_ref[0], down_ref[0]
    tail_columns = pl.ds(2 * MAIN, 2 * TAIL)
    nn = (((1,), (0,)), ((), ()))

    def middle(pre_gate, pre_up, grad_hidden):
        sig = jax.nn.sigmoid(pre_gate)
        activated = pre_gate * sig
        derivative = sig * (1.0 + pre_gate * (1.0 - sig))
        hidden = activated * pre_up
        grad_gate = grad_hidden * pre_up * derivative
        grad_up = grad_hidden * activated
        return hidden, grad_gate, grad_up

    x_main = x_ref[:, pl.ds(0, MAIN)]
    pre_gate = f32_dot(gate, x_main, nn)
    pre_up = f32_dot(up, x_main, nn)
    grad_hidden = f32_dot(down, x_ref[:, pl.ds(MAIN, MAIN)], nn)
    x_tail = x_ref[:, tail_columns]
    tail_gate = f32_dot(gate, x_tail, nn)
    tail_up = f32_dot(up, x_tail, nn)
    tail_grad = pltpu.roll(f32_dot(down, x_tail, nn), TAIL, 1)
    hidden, grad_gate, grad_up = middle(pre_gate, pre_up, grad_hidden)
    tail_hidden, tail_gg, tail_gu = middle(tail_gate, tail_up, tail_grad)
    first = lax.broadcasted_iota(jnp.int32, tail_hidden.shape, 1) < TAIL
    tail_hidden = jnp.where(first, tail_hidden, 0.0).astype(jnp.bfloat16)
    tail_gg = jnp.where(first, 0.0, pltpu.roll(tail_gg, TAIL, 1)).astype(jnp.bfloat16)
    tail_gu = jnp.where(first, 0.0, pltpu.roll(tail_gu, TAIL, 1)).astype(jnp.bfloat16)
    hidden = hidden.astype(jnp.bfloat16)
    grad_gate = grad_gate.astype(jnp.bfloat16)
    grad_up = grad_up.astype(jnp.bfloat16)

    block = 512

    @pl.loop(0, x_ref.shape[0] // block)
    def _(step):
        part = pl.ds(pl.multiple_of(step * block, block), block)
        g, u, d = gate_ref[0, :, part], up_ref[0, :, part], down_ref[0, :, part]
        y_ref[part, pl.ds(0, MAIN)] = f32_dot(d, hidden, TN).astype(jnp.bfloat16)
        y_ref[part, pl.ds(MAIN, MAIN)] = (f32_dot(g, grad_gate, TN) + f32_dot(u, grad_up, TN)).astype(jnp.bfloat16)
        tail = f32_dot(d, tail_hidden, TN) + f32_dot(g, tail_gg, TN) + f32_dot(u, tail_gu, TN)
        y_ref[part, tail_columns] = tail.astype(jnp.bfloat16)


def call(body, outs, *args, limit=None):
    return pl.pallas_call(
        body,
        out_shape=outs,
        compiler_params=pltpu.CompilerParams(vmem_limit_bytes=limit),
    )(*args)


def bf16(*shape):
    return jax.ShapeDtypeStruct(shape, jnp.bfloat16)


def shards(tokens, routes, gate_fixed, gate_weight, up_weight, down_weight, cotangent):
    routes_t, gate_t = routes.T, gate_fixed.T
    small = 24 * 2**20
    send = call(dispatch_body, bf16(BOTH, FEATURES), routes_t, gate_t, tokens.T, cotangent.T, limit=small)
    received = lax.all_to_all(send.reshape(EXPERTS, 2 * CAP, FEATURES), EP, 0, 0, tiled=True)
    columns = call(to_columns_body, bf16(FEATURES, BOTH), received.reshape(BOTH, FEATURES), limit=small)
    gathered = lax.all_gather(columns, ("z", "x"), axis=0, tiled=True)
    depth = gathered.shape[0]
    parts = call(expert_body, bf16(depth, BOTH), gathered, gate_weight, up_weight, down_weight, limit=48 * 2**20)
    parts = parts.reshape(8, 4, FEATURES, BOTH)
    summed = lax.psum_scatter(parts, "z", scatter_dimension=0, tiled=False)
    summed = lax.psum_scatter(summed, "x", scatter_dimension=0, tiled=False)
    back = call(to_rows_body, bf16(BOTH, FEATURES), summed, limit=small)
    home = lax.all_to_all(back.reshape(EXPERTS, 2 * CAP, FEATURES), EP, 0, 0, tiled=True)
    out, grad = call(
        combine_body,
        (bf16(FEATURES, TOKENS_HERE), bf16(FEATURES, TOKENS_HERE)),
        routes_t,
        gate_t,
        home.reshape(BOTH, FEATURES),
        limit=small,
    )
    return out.T, grad.T


def solution(mesh):
    fine = Mesh(mesh.devices.reshape(8, 2, 8, 4), ("y", "c", "z", "x"))
    ep, etp = EP, ("z", "x")
    placed = (P(ep, etp), P(ep, None), P(ep, None), P(ep, etp, None), P(ep, etp, None), P(ep, etp, None), P(ep, etp))
    return jax.shard_map(shards, mesh=fine, in_specs=placed, out_specs=(P(ep, etp), P(ep, etp)), check_vma=False)
```

time: 932 us -> 291 us (0.31)
  waiting for transfers between devices: 667 us -> 208 us
  local copies, waits for them, and re-layouts: 73.8 us -> 6.71 us
  blocking collectives: 86.4 us -> 42.7 us
  starting transfers between devices: 37.4 us -> 0.12 us
  other arithmetic: 32.2 us -> 0 us
  Pallas kernels: 0 us -> 19.7 us
  matrix products: 14.5 us -> 0 us
    unnamed x4 -> x3, waiting for transfers between devices: 415 us -> 0.05 us
    all_to_all x4 -> x0, waiting for transfers between devices: 252 us -> none  [the longest x1 80.7 us: shards(): lax.all_to_all(part_in.reshape(experts, capacity, -1), 'ep', split_axis=0...]
    reduce_scatter x0 -> x2, waiting for transfers between devices: none -> 111 us  [the longest x1 83.1 us: shards(): summed = lax.psum_scatter(parts, 'z', scatter_dimension=0, tiled=False)]
    all_gather x0 -> x1, waiting for transfers between devices: none -> 96.8 us  [shards(): gathered = lax.all_gather(columns, ('z', 'x'), axis=0, tiled=True)]
    all_gather x2 -> x0, blocking collectives: 86.4 us -> none  [the longest x1 44.5 us: shards(): features = lax.all_gather(tokens, 'etp', axis=1, tiled=True)]
    all_to_all x0 -> x2, blocking collectives: none -> 42.7 us  [the longest x1 21.8 us: shards(): lax.all_to_all(send.reshape(EXPERTS, 2 * CAP, FEATURES), EP, 0, 0, tiled=...]
    reshape x10 -> x0, local copies, waits for them, and re-layouts: 37.2 us -> none  [the longest x1 4.8 us: shards(): jnp.take(gradient_back.reshape(row_total, -1), target, axis=0)]
    all_to_all x4 -> x0, starting transfers between devices: 36.8 us -> none  [the longest x1 20.2 us: shards(): lax.all_to_all(outgoing, 'ep', split_axis=0, concat_axis=0, tiled=True)]
  transfers between devices with their start and end apart: 6 -> 3, of which waited for: 6 -> 3; matrix products, arithmetic and copies ran while one was open for 8% -> 0% of each run, Pallas kernels for 0% -> 0%
where the time goes in v1:
time: 291 us
  waiting for transfers between devices  208 us (71%)
  blocking collectives  42.7 us (15%)
  Pallas kernels  19.7 us (7%)
  between operations  13.8 us (5%)
  local copies, waits for them, and re-layouts  6.71 us (2%)
    all_gather x1, waiting for transfers between devices, shards(): gathered = lax.all_gather(columns, ('z', 'x'), axis=0, tiled=True)  96.8 us
    reduce_scatter x1, waiting for transfers between devices, shards(): summed = lax.psum_scatter(parts, 'z', scatter_dimension=0, tiled=False)  83.1 us
    reduce_scatter x1, waiting for transfers between devices, shards(): summed = lax.psum_scatter(summed, 'x', scatter_dimension=0, tiled=False)  27.7 us
    all_to_all x1, blocking collectives, shards(): lax.all_to_all(send.reshape(EXPERTS, 2 * CAP, FEATURES), EP, 0, 0, tiled=...  21.8 us
    all_to_all x1, blocking collectives, shards(): lax.all_to_all(back.reshape(EXPERTS, 2 * CAP, FEATURES), EP, 0, 0, tiled=...  20.9 us
    pallas_call x5, Pallas kernels, call(): pl.pallas_call(body, out_shape=outs, compiler_params=pltpu.CompilerParams...  19.7 us
    unnamed x20, local copies, waits for them, and re-layouts  6.71 us
  transfers between devices with their start and end apart: 3, of which 3 were waited for; matrix products, arithmetic and copies ran while one was open for 0% of the time, Pallas kernels for 0%

profile of v1, /device:TPU:1, one launch (start us, length us, event | category | flops | bytes accessed | tf_op | source)
XLA Modules:
  0.0 290.7 jit_solution(12376134910593154281)
XLA Ops:
  7.2 0.0 copy-start
  7.2 0.0 all-gather.2.cloned.1.call-start
  7.2 0.0 copy-start.4
  7.2 0.8 copy-done.4
  8.1 0.0 copy-start.5
  8.1 0.7 copy-done.5
  8.8 0.0 copy-start.6
  8.8 0.7 copy-done.6
  9.5 0.0 copy-start.8
  9.5 0.7 copy-done.8
  10.2 0.7 shard_map.86
  10.8 21.8 %all_to_all.10 = bf16[16,72,96]{2,1,0:T(8,128)(2,1)S(1)} all-to-all(bf16[16,72,96]{2,1,0:T(8,128)(2,1)S(1)} %bitcast.14), channel_id=1, replica_groups=mesh['y'=8,'c'=2,'z'=8,'x'=4] {'y','c'}, dimensions={0} | all-to-all | bytes 442368 | tf_op jit(solution)/shard_map/all_to_all | solution.py:163
  32.6 1.7 shard_map.87
  34.3 0.0 all-gather.2.cloned.1.call-update
  34.3 0.0 reduce-scatter.3.cloned.1.call-start
  34.4 96.8 %all-gather.2.cloned.1.call-done.x_ref = bf16[3072,1152]{1,0:T(8,128)(2,1)} async-done(((bf16[96,1152]{1,0:T(8,128)(2,1)}), bf16[3072,1152]{1,0:T(8,128)(2,1)}) %all-gather.2.cloned.1.call-update) | async-done | bytes 7077904 | tf_op jit(solution)/shard_map/all_gather | solution.py:165
  131.1 0.0 copy-done
  131.1 0.0 copy-start.1
  131.1 1.4 copy-done.1
  132.6 0.0 copy-start.2
  132.6 1.4 copy-done.2
  134.0 15.1 %shard_map.88 = bf16[3072,1152]{1,0:T(8,128)(2,1)} custom-call(bf16[3072,1152]{1,0:T(8,128)(2,1)} %all-gather.2.cloned.1.call-done.x_ref, bf16[1,256,3072]{2,1,0:T(8,128)(2,1)S(1)} %copy-done, bf16[1,256,3072]{2,1,0:T(8,128)(2,1)S(1)} %copy-done.1, bf16[1,256,3072]{2,1,0:T(8,128)(2,1)S(1)} %copy-done.2), custom_call_target="tpu_custom_call" | custom-call | tf_op jit(solution)/shard_map/pallas_call | solution.py:148
  149.1 0.0 reduce-scatter.3.cloned.1.call-update
  149.1 0.0 copy-start.7
  149.1 0.0 copy-start.9
  149.1 0.0 reduce-scatter.5.cloned.1.call-start
  149.2 83.1 %reduce-scatter.3.cloned.1.call-done = bf16[1,4,96,1152]{3,2,1,0:T(8,128)(2,1)} async-done(((bf16[8,4,96,1152]{3,2,1,0:T(8,128)(2,1)}), bf16[1,4,96,1152]{3,2,1,0:T(8,128)(2,1)}) %reduce-scatter.3.cloned.1.call-update) | async-done | bytes 884752 | tf_op jit(solution)/shard_map/reduce_scatter | solution.py:169
  232.2 0.0 reduce-scatter.5.cloned.1.call-update
  232.3 27.7 %reduce-scatter.5.cloned.1.call-done = bf16[1,96,1152]{2,1,0:T(8,128)(2,1)} async-done(((bf16[4,96,1152]{2,1,0:T(8,128)(2,1)}), bf16[1,96,1152]{2,1,0:T(8,128)(2,1)}) %reduce-scatter.5.cloned.1.call-update) | async-done | bytes 221200 | tf_op jit(solution)/shard_map/reduce_scatter | solution.py:170
  260.0 0.0 copy-start.3
  260.0 0.9 copy-done.3
  260.9 1.0 shard_map.89
  261.9 20.9 %all_to_all.11 = bf16[16,72,96]{2,1,0:T(8,128)(2,1)S(1)} all-to-all(bf16[16,72,96]{2,1,0:T(8,128)(2,1)S(1)} %bitcast.16), channel_id=1, replica_groups=mesh['y'=8,'c'=2,'z'=8,'x'=4] {'y','c'}, dimensions={0} | all-to-all | bytes 442368 | tf_op jit(solution)/shard_map/all_to_all | solution.py:172
  282.9 0.0 copy-done.7
  282.9 0.0 copy-done.9
  282.9 1.3 shard_map.90
Async XLA Ops:
  7.2 124.0 %copy-start = (bf16[1,256,3072]{2,1,0:T(8,128)(2,1)S(1)}, bf16[1,256,3072]{2,1,0:T(8,128)(2,1)}, u32[]{:S(2)}) copy-start(bf16[1,256,3072]{2,1,0:T(8,128)(2,1)} %gate_ref.1) | copy-start | bytes 4718596
  7.2 124.0 %all-gather.2.cloned.1.call-start = ((), (), s32[]{:S(2)}) async-start(), calls=%async_computation.4 | async-start | bytes 7299072 | tf_op jit(solution)/shard_map/all_gather | solution.py:165
  7.2 0.8 copy-start.4
  8.1 0.7 copy-start.5
  8.8 0.7 copy-start.6
  9.5 0.7 copy-start.8
  34.3 197.9 %reduce-scatter.3.cloned.1.call-start = ((), (), s32[]{:S(2)}) async-start(), calls=%async_computation.5 | async-start | bytes 7962624 | tf_op jit(solution)/shard_map/reduce_scatter | solution.py:169
  131.1 1.4 copy-start.1
  132.6 1.4 copy-start.2
  149.1 133.8 %copy-start.7 = (s32[128,4]{0,1:T(4,128)S(1)}, s32[128,4]{0,1:T(4,128)}, u32[]{:S(2)}) copy-start(s32[128,4]{0,1:T(4,128)} %param.8) | copy-start | bytes 6148
  149.1 133.8 %copy-start.9 = (s32[128,4]{0,1:T(4,128)S(1)}, s32[128,4]{0,1:T(4,128)}, u32[]{:S(2)}) copy-start(s32[128,4]{0,1:T(4,128)} %param.9) | copy-start | bytes 6148
  149.1 110.9 %reduce-scatter.5.cloned.1.call-start = ((), (), s32[]{:S(2)}) async-start(), calls=%async_computation.6 | async-start | bytes 1105920 | tf_op jit(solution)/shard_map/reduce_scatter | solution.py:170
  260.0 0.9 copy-start.3
Sparse Core Ops, SparseCore 0:
  34.4 96.6 all-gather.1
  149.2 82.9 reduce-scatter.2
  235.1 24.8 reduce-scatter.4

commit v2 on v1

v2 whole, which is shorter than its diff:
```python
import jax
import jax.numpy as jnp
from jax import lax
from jax.experimental import pallas as pl
from jax.experimental.pallas import tpu as pltpu
from jax.sharding import Mesh
from jax.sharding import PartitionSpec as P

EXPERTS = 16
CAP = 36
TOKENS_HERE = 128
FEATURES = 96
ROWS = EXPERTS * CAP
MAIN = 512
TAIL = ROWS - MAIN
WIDE = MAIN + 2 * TAIL
NEAR = 384
PLANES = 8
STEP = 4 * FEATURES
DEPTH = PLANES * STEP
EP = ("y", "c")
ETP = ("z", "x")
RIGHT = [(0, 1), (1, 2), (2, 3), (3, 0)]
LEFT = [(1, 0), (2, 1), (3, 2), (0, 3)]
NT = (((1,), (1,)), ((), ()))
TN = (((0,), (0,)), ((), ()))
NN = (((1,), (0,)), ((), ()))


def f32_dot(a, b, dims):
    return lax.dot_general(a, b, dims, preferred_element_type=jnp.float32)


def slots(routes, gate_fixed):
    named = []
    gates = []
    for e in range(EXPERTS):
        hit = routes == e
        named.append(jnp.sum(hit.astype(jnp.float32), axis=0, keepdims=True))
        gates.append(jnp.sum(jnp.where(hit, gate_fixed, 0).astype(jnp.float32), axis=0, keepdims=True))
    member = jnp.concatenate(named, axis=0)
    before = lax.broadcasted_iota(jnp.int32, (TOKENS_HERE, TOKENS_HERE), 0)
    after = lax.broadcasted_iota(jnp.int32, (TOKENS_HERE, TOKENS_HERE), 1)
    earlier = (before < after).astype(jnp.bfloat16)
    rank = jnp.dot(member.astype(jnp.bfloat16), earlier, preferred_element_type=jnp.float32)
    rank = jnp.where(member > 0.0, rank, -1.0)
    slot = lax.broadcasted_iota(jnp.int32, (CAP, TOKENS_HERE), 0).astype(jnp.float32)
    onehot = [(rank[e : e + 1] == slot).astype(jnp.float32) for e in range(EXPERTS)]
    return onehot, gates


def dispatch_body(routes_ref, gate_ref, tokens_ref, cot_ref, out_ref):
    onehot, gates = slots(routes_ref[...], gate_ref[...])
    values = jnp.concatenate([tokens_ref[...], cot_ref[...]], axis=0)
    is_token = lax.broadcasted_iota(jnp.int32, (CAP, 2 * FEATURES), 1) < FEATURES
    for e in range(EXPERTS):
        scale = jnp.sum(onehot[e] * gates[e], axis=1, keepdims=True) * (1.0 / 65536.0)
        rows = f32_dot(onehot[e].astype(jnp.bfloat16), values, NT)
        out_ref[e] = (rows * jnp.where(is_token, 1.0, scale)).astype(jnp.bfloat16)


def place_of(source):
    slot = lax.broadcasted_iota(jnp.int32, (CAP, MAIN + 2 * TAIL), 0)
    number = lax.broadcasted_iota(jnp.int32, (CAP, MAIN + 2 * TAIL), 1)
    return (number == slot + source * CAP).astype(jnp.bfloat16)


def columns_body(rows_ref, first_ref, second_ref):
    total = jnp.zeros((2 * FEATURES, MAIN + 2 * TAIL), jnp.float32)
    for source in range(EXPERTS):
        total = total + f32_dot(rows_ref[source], place_of(source), TN)
    tokens, cotangent = total[:FEATURES], total[FEATURES:]
    first_ref[...] = tokens[:, :MAIN].astype(jnp.bfloat16)
    second_ref[:, pl.ds(0, MAIN)] = cotangent[:, :MAIN].astype(jnp.bfloat16)
    low = lax.broadcasted_iota(jnp.int32, (FEATURES, 2 * TAIL), 1) < TAIL
    tail = jnp.where(low, tokens[:, MAIN:], pltpu.roll(cotangent[:, MAIN:], TAIL, 1))
    second_ref[:, pl.ds(MAIN, 2 * TAIL)] = tail.astype(jnp.bfloat16)


def total_of(ref):
    total = ref[0].astype(jnp.float32)
    for k in range(1, ref.shape[0]):
        total = total + ref[k].astype(jnp.float32)
    return total


def rows_body(first_ref, second_ref, third_ref, out_ref):
    first = total_of(first_ref)
    second = jnp.concatenate([total_of(second_ref), total_of(third_ref)], axis=1)
    tail = second[:, MAIN:]
    low = lax.broadcasted_iota(jnp.int32, tail.shape, 1) < TAIL
    outs = jnp.concatenate([first, jnp.where(low, tail, 0.0)], axis=1)
    grads = jnp.concatenate([second[:, :MAIN], jnp.where(low, pltpu.roll(tail, TAIL, 1), 0.0)], axis=1)
    both = jnp.concatenate([outs, grads], axis=0).astype(jnp.bfloat16)
    for source in range(EXPERTS):
        out_ref[source] = f32_dot(place_of(source), both, NT).astype(jnp.bfloat16)


def combine_body(routes_ref, gate_ref, rows_ref, out_ref, grad_ref):
    onehot, gates = slots(routes_ref[...], gate_ref[...])
    total = jnp.zeros((2 * FEATURES, 3 * TOKENS_HERE), jnp.float32)
    for e in range(EXPERTS):
        high = jnp.floor(gates[e] * (1.0 / 256.0))
        low = gates[e] - 256.0 * high
        factors = jnp.concatenate([onehot[e] * high, onehot[e] * low, onehot[e]], axis=1).astype(jnp.bfloat16)
        total = total + f32_dot(rows_ref[e], factors, TN)
    by_high, by_low = total[:FEATURES, :TOKENS_HERE], total[:FEATURES, TOKENS_HERE : 2 * TOKENS_HERE]
    out_ref[...] = (by_high * (1.0 / 256.0) + by_low * (1.0 / 65536.0)).astype(jnp.bfloat16)
    grad_ref[...] = total[FEATURES:, 2 * TOKENS_HERE :].astype(jnp.bfloat16)


def activation(pre_gate, pre_up):
    sig = jax.nn.sigmoid(pre_gate)
    activated = pre_gate * sig
    derivative = sig * (1.0 + pre_gate * (1.0 - sig))
    return activated * pre_up, pre_up * derivative, activated


def start_all(copies):
    for copy in copies:
        copy.start()


def wait_all(copies):
    for copy in copies:
        copy.wait()


def forward_body(x_ref, gate_ref, up_ref, down_ref, y_ref, to_gate_ref, to_up_ref, x, gate, up, down, y, sems, out_sems):
    loads = [
        pltpu.make_async_copy(source, target, sems.at[number])
        for number, (source, target) in enumerate(((x_ref, x), (gate_ref, gate), (up_ref, up), (down_ref, down)))
    ]
    start_all(loads)
    wait_all(loads[:2])
    pre_gate = f32_dot(gate[0], x[...], NN)
    loads[2].wait()
    hidden, to_gate, to_up = activation(pre_gate, f32_dot(up[0], x[...], NN))
    to_gate_ref[...] = to_gate
    to_up_ref[...] = to_up
    hidden = hidden.astype(jnp.bfloat16)
    loads[3].wait()
    stores = []
    for step in range(PLANES):
        y[step] = f32_dot(down[0, :, pl.ds(step * STEP, STEP)], hidden, TN).astype(jnp.bfloat16)
        stores.append(pltpu.make_async_copy(y.at[step], y_ref.at[step], out_sems.at[step]))
        stores[-1].start()
    wait_all(stores)


def backward_body(
    x_index,
    own,
    left,
    right,
    far_low,
    far_high,
    to_gate_ref,
    to_up_ref,
    gate_ref,
    up_ref,
    down_ref,
    y_ref,
    z_ref,
    x_ref,
    gate,
    up,
    down,
    y,
    z,
    sems,
    y_sems,
    z_sems,
):
    me = x_index[0]
    whole, low, high = pl.ds(0, 8), pl.ds(0, 4), pl.ds(4, 4)
    pieces = ((own, whole, 0), (left, whole, 3), (right, whole, 1), (far_low, low, 2), (far_high, high, 2))
    loads = [pltpu.make_async_copy(down_ref, down, sems.at[5])]
    for number, (source, planes, away) in enumerate(pieces):
        target = x_ref.at[planes, lax.rem(me + away, 4)]
        loads.append(pltpu.make_async_copy(source, target, sems.at[number]))
    loads.append(pltpu.make_async_copy(gate_ref, gate, sems.at[6]))
    loads.append(pltpu.make_async_copy(up_ref, up, sems.at[7]))
    start_all(loads)
    wait_all(loads[:6])
    x = x_ref[...].reshape(DEPTH, WIDE)
    tail = x[:, MAIN:]
    grad_hidden = f32_dot(down[0], x, NN)
    wait_all(loads[6:])
    tail_hidden, tail_to_gate, tail_to_up = activation(f32_dot(gate[0], tail, NN), f32_dot(up[0], tail, NN))
    tail_grad = grad_hidden[:, MAIN:]
    grad_hidden = grad_hidden[:, :MAIN]
    is_low = lax.broadcasted_iota(jnp.int32, tail_grad.shape, 1) < TAIL
    tail_hidden = jnp.where(is_low, tail_hidden, 0.0).astype(jnp.bfloat16)
    tail_gate = jnp.where(is_low, 0.0, tail_grad * pltpu.roll(tail_to_gate, TAIL, 1)).astype(jnp.bfloat16)
    tail_up = jnp.where(is_low, 0.0, tail_grad * pltpu.roll(tail_to_up, TAIL, 1)).astype(jnp.bfloat16)
    grad_gate = jnp.concatenate([(grad_hidden * to_gate_ref[...]).astype(jnp.bfloat16), tail_gate], axis=1)
    grad_up = jnp.concatenate([(grad_hidden * to_up_ref[...]).astype(jnp.bfloat16), tail_up], axis=1)
    stores = []
    for step in range(PLANES):
        part = pl.ds(step * STEP, STEP)
        value = f32_dot(gate[0, :, part], grad_gate, TN) + f32_dot(up[0, :, part], grad_up, TN)
        out = f32_dot(down[0, :, part], tail_hidden, TN)
        y[step] = value[:, :NEAR].astype(jnp.bfloat16)
        rest = jnp.concatenate([value[:, NEAR:MAIN], value[:, MAIN:] + out], axis=1)
        z[:, step] = rest.astype(jnp.bfloat16).reshape(4, FEATURES, WIDE - NEAR)
        stores.append(pltpu.make_async_copy(y.at[step], y_ref.at[step], y_sems.at[step]))
        stores.append(pltpu.make_async_copy(z.at[:, step], z_ref.at[:, step], z_sems.at[step]))
        start_all(stores[-2:])
    wait_all(stores)


def call(body, outs, *args, specs=None, out_specs=None, scratch=(), limit=24):
    vmem = pl.BlockSpec(memory_space=pltpu.VMEM)
    return pl.pallas_call(
        body,
        out_shape=outs,
        in_specs=specs or [vmem] * len(args),
        out_specs=out_specs or jax.tree.map(lambda _: vmem, outs),
        scratch_shapes=scratch,
        compiler_params=pltpu.CompilerParams(vmem_limit_bytes=limit * 2**20),
    )(*args)


def bf16(*shape):
    return jax.ShapeDtypeStruct(shape, jnp.bfloat16)


def shards(tokens, routes, gate_fixed, gate_weight, up_weight, down_weight, cotangent):
    named = (routes.T, gate_fixed.T)
    weights = (gate_weight, up_weight, down_weight)
    send = call(dispatch_body, bf16(EXPERTS, CAP, 2 * FEATURES), *named, tokens.T, cotangent.T)
    received = lax.all_to_all(send, EP, 0, 0, tiled=True)
    first, second = call(columns_body, (bf16(FEATURES, MAIN), bf16(FEATURES, WIDE)), received)

    first = lax.all_gather(first, "x", axis=0, tiled=True)
    first, second = lax.optimization_barrier((first, second))
    first = lax.all_gather(first, "z", axis=0, tiled=True)
    own = lax.all_gather(second, "z", axis=0, tiled=False)
    left = lax.ppermute(own, "x", RIGHT)
    right = lax.ppermute(own, "x", LEFT)
    first, left, right = lax.optimization_barrier((first, left, right))
    vmem, hbm = pl.BlockSpec(memory_space=pltpu.VMEM), pl.BlockSpec(memory_space=pltpu.HBM)
    weight = pltpu.VMEM(gate_weight.shape, jnp.bfloat16)
    semaphores = pltpu.SemaphoreType.DMA((8,))
    scale = jax.ShapeDtypeStruct((gate_weight.shape[1], MAIN), jnp.float32)
    y_first, to_gate, to_up = call(
        forward_body,
        (bf16(PLANES, STEP, MAIN), scale, scale),
        first,
        *weights,
        specs=[hbm] * 4,
        out_specs=(hbm, vmem, vmem),
        scratch=[pltpu.VMEM((DEPTH, MAIN), jnp.bfloat16)]
        + [weight] * 3
        + [pltpu.VMEM((PLANES, STEP, MAIN), jnp.bfloat16), semaphores, semaphores],
        limit=56,
    )
    left, right, to_gate = lax.optimization_barrier((left, right, to_gate))
    far_low = lax.ppermute(left[:4], "x", RIGHT)
    far_high = lax.ppermute(right[4:], "x", LEFT)
    y_first = lax.psum_scatter(y_first, "z", scatter_dimension=0, tiled=False)
    y_second, y_third = call(
        backward_body,
        (bf16(PLANES, STEP, NEAR), bf16(4, PLANES, FEATURES, WIDE - NEAR)),
        lax.axis_index("x").astype(jnp.int32).reshape(1),
        own,
        left,
        right,
        far_low,
        far_high,
        to_gate,
        to_up,
        *weights,
        specs=[pl.BlockSpec(memory_space=pltpu.SMEM)] + [hbm] * 5 + [vmem] * 2 + [hbm] * 3,
        out_specs=(hbm, hbm),
        scratch=[pltpu.VMEM((PLANES, 4, FEATURES, WIDE), jnp.bfloat16)]
        + [weight] * 3
        + [
            pltpu.VMEM((PLANES, STEP, NEAR), jnp.bfloat16),
            pltpu.VMEM((4, PLANES, FEATURES, WIDE - NEAR), jnp.bfloat16),
            semaphores,
            semaphores,
            semaphores,
        ],
        limit=56,
    )
    y_second = lax.psum_scatter(y_second, "z", scatter_dimension=0, tiled=False)
    y_third = lax.all_to_all(y_third, "x", 0, 0, tiled=True)
    y_third = jnp.sum(y_third.astype(jnp.float32), axis=0).astype(jnp.bfloat16)
    y_third = lax.all_to_all(y_third, "z", 0, 0, tiled=True)
    y_first = lax.all_to_all(y_first.reshape(4, FEATURES, MAIN), "x", 0, 0, tiled=True)
    y_first, y_third, y_second = lax.optimization_barrier((y_first, y_third, y_second))
    y_second = lax.all_to_all(y_second.reshape(4, FEATURES, NEAR), "x", 0, 0, tiled=True)

    back = call(rows_body, bf16(EXPERTS, CAP, 2 * FEATURES), y_first, y_second, y_third)
    home = lax.all_to_all(back, EP, 0, 0, tiled=True)
    out, grad = call(combine_body, (bf16(FEATURES, TOKENS_HERE), bf16(FEATURES, TOKENS_HERE)), *named, home)
    return out.T, grad.T


def solution(mesh):
    fine = Mesh(mesh.devices.reshape(8, 2, 8, 4), ("y", "c", "z", "x"))
    ep, etp = EP, ETP
    placed = (P(ep, etp), P(ep, None), P(ep, None), P(ep, etp, None), P(ep, etp, None), P(ep, etp, None), P(ep, etp))
    return jax.shard_map(shards, mesh=fine, in_specs=placed, out_specs=(P(ep, etp), P(ep, etp)), check_vma=False)
```

time: 291 us -> 245 us (0.84)
  waiting for transfers between devices: 208 us -> 54.2 us
  blocking collectives: 42.7 us -> 131 us
  starting transfers between devices: 0.12 us -> 16.7 us
    all_gather x1, waiting for transfers between devices: 96.8 us -> 3.11 us  [shards(): first = lax.all_gather(first, 'z', axis=0, tiled=True)]
    reduce_scatter x2, waiting for transfers between devices: 111 us -> 28.6 us  [the longest x1 28.6 us: shards(): y_second = lax.psum_scatter(y_second, 'z', scatter_dimension=0, tiled=False)]
    all_to_all x2 -> x5, blocking collectives: 42.7 us -> 89.6 us  [the longest x1 25.9 us: shards(): home = lax.all_to_all(back, EP, 0, 0, tiled=True)]
    all_gather x0 -> x2, blocking collectives: none -> 41.4 us  [the longest x1 29.9 us: shards(): own = lax.all_gather(second, 'z', axis=0, tiled=False)]
    ppermute x0 -> x4, waiting for transfers between devices: none -> 22.4 us  [the longest x1 13.7 us: shards(): left = lax.ppermute(own, 'x', RIGHT)]
    ppermute x0 -> x4, starting transfers between devices: none -> 13 us  [the longest x1 3.63 us: shards(): far_high = lax.ppermute(right[4:], 'x', LEFT)]
    all_to_all x0 -> x1, starting transfers between devices: none -> 3.59 us  [shards(): lax.all_to_all(y_first.reshape(4, FEATURES, MAIN), 'x', 0, 0, tiled=True)]
    pallas_call x5 -> x6, Pallas kernels: 19.7 us -> 22.5 us  [call(): pl.pallas_call(body, out_shape=outs, in_specs=specs or [vmem] * len(args)...]
  transfers between devices with their start and end apart: 3 -> 8, of which waited for: 3 -> 6; matrix products, arithmetic and copies ran while one was open for 0% -> 0% of each run, Pallas kernels for 0% -> 4%
where the time goes in v2:
time: 245 us; the launch traced here: 244 us
  blocking collectives  131 us (53%)
  waiting for transfers between devices  54.2 us (22%)
  Pallas kernels  22.5 us (9%)
  starting transfers between devices  16.7 us (7%)
  between operations  13.9 us (6%)
  local copies, waits for them, and re-layouts  5.88 us (2%)
    all_gather x1, blocking collectives, shards(): own = lax.all_gather(second, 'z', axis=0, tiled=False)  29.9 us
    reduce_scatter x1, waiting for transfers between devices, shards(): y_second = lax.psum_scatter(y_second, 'z', scatter_dimension=0, tiled=False)  28.6 us
    all_to_all x1, blocking collectives, shards(): home = lax.all_to_all(back, EP, 0, 0, tiled=True)  25.9 us
    pallas_call x6, Pallas kernels, call(): pl.pallas_call(body, out_shape=outs, in_specs=specs or [vmem] * len(args)...  22.5 us
    all_to_all x1, blocking collectives, shards(): received = lax.all_to_all(send, EP, 0, 0, tiled=True)  22.3 us
    all_to_all x1, blocking collectives, shards(): y_third = lax.all_to_all(y_third, 'x', 0, 0, tiled=True)  18.3 us
    ppermute x1, waiting for transfers between devices, shards(): left = lax.ppermute(own, 'x', RIGHT)  13.7 us
    all_to_all x1, blocking collectives, shards(): y_third = lax.all_to_all(y_third, 'z', 0, 0, tiled=True)  13.5 us
  transfers between devices with their start and end apart: 8, of which 6 were waited for; matrix products, arithmetic and copies ran while one was open for 0% of the time, Pallas kernels for 4%

profile of v2, /device:TPU:1, one launch (start us, length us, event | category | flops | bytes accessed | tf_op | source)
XLA Modules:
  0.0 244.5 jit_solution(2160524452024625324)
XLA Ops:
  7.2 0.0 all-gather.3.cloned.1.call-start
  7.2 0.0 copy-start
  7.2 0.7 copy-done
  7.9 0.0 copy-start.1
  8.0 0.7 copy-done.1
  8.7 0.7 copy-done.2
  9.4 0.7 copy-done.4
  10.1 0.7 shard_map.86
  10.8 22.3 %all_to_all.30.rows_ref = bf16[16,36,192]{2,1,0:T(8,128)(2,1)S(1)} all-to-all(bf16[16,36,192]{2,1,0:T(8,128)(2,1)S(1)} %shard_map.86), channel_id=1, replica_groups=mesh['y'=8,'c'=2,'z'=8,'x'=4] {'y','c'}, dimensions={0} | all-to-all | bytes 442368 | tf_op jit(solution)/shard_map/all_to_all | solution.py:233
  33.1 1.0 shard_map.87
  34.1 11.5 %all_gather.12 = bf16[384,512]{1,0:T(8,128)(2,1)} all-gather(bf16[96,512]{1,0:T(8,128)(2,1)S(1)} %get-tuple-element.22), channel_id=1, replica_groups=mesh['y'=8,'c'=2,'z'=8,'x'=4] {'x'}, dimensions={0}, use_global_device_ids=true | all-gather | bytes 491520 | tf_op jit(solution)/shard_map/all_gather | solution.py:236
  45.6 0.0 all-gather.3.cloned.1.call-update
  45.6 0.0 reduce-scatter.3.cloned.1.call-start
  45.7 29.9 %all-gather = bf16[768,640]{1,0:T(8,128)(2,1)S(1)} all-gather(bf16[96,640]{1,0:T(8,128)(2,1)S(1)} %get-tuple-element.25), channel_id=2, replica_groups=mesh['y'=8,'c'=2,'z'=8,'x'=4] {'z'}, dimensions={0}, use_global_device_ids=true | all-gather | bytes 1105920 | tf_op jit(solution)/shard_map/all_gather | solution.py:239
  75.6 3.1 %collective-permute-start = (bf16[8,96,640]{2,1,0:T(8,128)(2,1)S(1)}, bf16[8,96,640]{2,1,0:T(8,128)(2,1)S(1)}, u32[]{:S(2)}, u32[]{:S(2)}) collective-permute-start(bf16[8,96,640]{2,1,0:T(8,128)(2,1)S(1)} %bitcast.17), channel_id=1, source_target_pairs={{0,1},{1,2},{2,3},{3,0},{4,5},{5,6},{6,7},{7,4},{8,9},{9,10},{10,1... | collective-permute-start | bytes 2949128 | tf_op jit(solution)/shard_map/ppermute | solution.py:240
  78.7 3.4 %collective-permute-start.1 = (bf16[8,96,640]{2,1,0:T(8,128)(2,1)S(1)}, bf16[8,96,640]{2,1,0:T(8,128)(2,1)S(1)}, u32[]{:S(2)}, u32[]{:S(2)}) collective-permute-start(bf16[8,96,640]{2,1,0:T(8,128)(2,1)S(1)} %bitcast.18), channel_id=1, source_target_pairs={{1,0},{2,1},{3,2},{0,3},{5,4},{6,5},{7,6},{4,7},{9,8},{10,9},{11,1... | collective-permute-start | bytes 2949128 | tf_op jit(solution)/shard_map/ppermute | solution.py:241
  82.1 13.7 %collective-permute-done.left = bf16[8,96,640]{2,1,0:T(8,128)(2,1)S(1)} collective-permute-done((bf16[8,96,640]{2,1,0:T(8,128)(2,1)S(1)}, bf16[8,96,640]{2,1,0:T(8,128)(2,1)S(1)}, u32[]{:S(2)}, u32[]{:S(2)}) %collective-permute-start) | collective-permute-done | bytes 983072 | tf_op jit(solution)/shard_map/ppermute | solution.py:240
  95.8 1.9 collective-permute-done.1.right
  97.7 3.1 %all-gather.3.cloned.1.call-done.x_ref = bf16[3072,512]{1,0:T(8,128)(2,1)} async-done(((bf16[384,512]{1,0:T(8,128)(2,1)}), bf16[3072,512]{1,0:T(8,128)(2,1)}) %all-gather.3.cloned.1.call-update) | async-done | bytes 3145744 | tf_op jit(solution)/shard_map/all_gather | solution.py:238
  100.8 7.4 %shard_map.88 = (bf16[8,384,512]{2,1,0:T(8,128)(2,1)}, f32[256,512]{1,0:T(8,128)}, f32[256,512]{1,0:T(8,128)}) custom-call(bf16[3072,512]{1,0:T(8,128)(2,1)} %all-gather.3.cloned.1.call-done.x_ref, bf16[1,256,3072]{2,1,0:T(8,128)(2,1)} %gate_ref.3, bf16[1,256,3072]{2,1,0:T(8,128)(2,1)} %up_ref.3, bf16[1,256,3072]{2,1,0:T(8,128)(2,1)} %down_ref.3), custom_call_target="tpu_custom_call" | custom-call | tf_op jit(solution)/shard_map/pallas_call | solution.py:215
  108.2 0.0 copy-done.6
  108.2 0.0 reduce-scatter.3.cloned.1.call-update
  108.2 0.0 reduce-scatter.5.cloned.1.call-start
  108.3 0.0 copy-done.7
  108.3 0.8 slice.6
  109.1 2.9 %collective-permute-start.2 = (bf16[4,96,640]{2,1,0:T(8,128)(2,1)}, bf16[4,96,640]{2,1,0:T(8,128)(2,1)S(1)}, u32[]{:S(2)}, u32[]{:S(2)}) collective-permute-start(bf16[4,96,640]{2,1,0:T(8,128)(2,1)} %slice.6), channel_id=1, source_target_pairs={{0,1},{1,2},{2,3},{3,0},{4,5},{5,6},{6,7},{7,4},{8,9},{9,10},{10,1... | collective-permute-start | bytes 1474568 | tf_op jit(solution)/shard_map/ppermute | solution.py:260
  112.0 0.0 copy-done.8
  112.0 3.6 %collective-permute-start.3 = (bf16[4,96,640]{2,1,0:T(8,128)(2,1)S(1)}, bf16[4,96,640]{2,1,0:T(8,128)(2,1)S(1)}, u32[]{:S(2)}, u32[]{:S(2)}) collective-permute-start(bf16[4,96,640]{2,1,0:T(8,128)(2,1)S(1)} %slice.7), channel_id=1, source_target_pairs={{1,0},{2,1},{3,2},{0,3},{5,4},{6,5},{7,6},{4,7},{9,8},{10,9},{11,1... | collective-permute-start | bytes 1474568 | tf_op jit(solution)/shard_map/ppermute | solution.py:261
  115.7 5.1 %collective-permute-done.2.far_low = bf16[4,96,640]{2,1,0:T(8,128)(2,1)S(1)} collective-permute-done((bf16[4,96,640]{2,1,0:T(8,128)(2,1)}, bf16[4,96,640]{2,1,0:T(8,128)(2,1)S(1)}, u32[]{:S(2)}, u32[]{:S(2)}) %collective-permute-start.2) | collective-permute-done | bytes 491552 | tf_op jit(solution)/shard_map/ppermute | solution.py:260
  120.8 1.8 collective-permute-done.3.far_high
  122.6 0.0 copy-done.10
  122.6 0.8 copy-done.11
  123.3 10.2 %shard_map.89 = (bf16[8,384,384]{2,1,0:T(8,128)(2,1)}, bf16[4,8,96,256]{3,2,1,0:T(8,128)(2,1)}) custom-call(s32[1]{0:T(128)} %bitcast.6.x_index, bf16[8,96,640]{2,1,0:T(8,128)(2,1)} %bitcast.19, bf16[8,96,640]{2,1,0:T(8,128)(2,1)} %copy-done.7, bf16[8,96,640]{2,1,0:T(8,128)(2,1)} %copy-done.8, bf16[4,96,640]{2,1,0:T(8,128)(2,1)} %copy-done.10, ...), custom_call_target="tpu_custom_call" | custom-call | tf_op jit(solution)/shard_map/pallas_call | solution.py:215
  133.6 0.0 copy-start.9
  133.6 0.0 reduce-scatter.5.cloned.1.call-update
  133.6 1.4 copy-done.9
  135.0 18.3 %all_to_all.31 = bf16[4,8,96,256]{3,2,1,0:T(8,128)(2,1)S(1)} all-to-all(bf16[4,8,96,256]{3,2,1,0:T(8,128)(2,1)S(1)} %copy-done.9), channel_id=1, replica_groups=mesh['y'=8,'c'=2,'z'=8,'x'=4] {'x'}, dimensions={0} | all-to-all | bytes 3145728 | tf_op jit(solution)/shard_map/all_to_all | solution.py:289
  153.3 0.3 reduce_sum.12
  153.6 13.5 %all_to_all.32.third_ref = bf16[8,96,256]{2,1,0:T(8,128)(2,1)S(1)} all-to-all(bf16[8,96,256]{2,1,0:T(8,128)(2,1)S(1)} %reduce_sum.12), channel_id=1, replica_groups=mesh['y'=8,'c'=2,'z'=8,'x'=4] {'z'}, dimensions={0} | all-to-all | bytes 786432 | tf_op jit(solution)/shard_map/all_to_all | solution.py:291
  167.1 3.6 %all-to-all-start.1 = ((bf16[4,96,512]{2,1,0:T(8,128)(2,1)}), bf16[4,96,512]{2,1,0:T(8,128)(2,1)S(1)}, u32[]{:S(2)}, u32[]{:S(2)}) async-start(bf16[4,96,512]{2,1,0:T(8,128)(2,1)} %bitcast.20), calls=%async_computation.2 | async-start | bytes 786432 | tf_op jit(solution)/shard_map/all_to_all | solution.py:292
  170.7 28.6 %reduce-scatter.5.cloned.1.call-done = bf16[1,384,384]{2,1,0:T(8,128)(2,1)} async-done(((bf16[8,384,384]{2,1,0:T(8,128)(2,1)}), bf16[1,384,384]{2,1,0:T(8,128)(2,1)}) %reduce-scatter.5.cloned.1.call-update) | async-done | bytes 294928 | tf_op jit(solution)/shard_map/reduce_scatter | solution.py:288
  199.3 0.0 all-to-all-done.1.first_ref
  199.3 9.6 %all_to_all.33.second_ref = bf16[4,96,384]{2,1,0:T(8,128)(2,1)S(1)} all-to-all(bf16[4,96,384]{2,1,0:T(8,128)(2,1)} %bitcast.21), channel_id=1, replica_groups=mesh['y'=8,'c'=2,'z'=8,'x'=4] {'x'}, dimensions={0} | all-to-all | bytes 589824 | tf_op jit(solution)/shard_map/all_to_all | solution.py:294
  208.9 1.6 shard_map.90
  210.5 25.9 %all_to_all.34.rows_ref = bf16[16,36,192]{2,1,0:T(8,128)(2,1)S(1)} all-to-all(bf16[16,36,192]{2,1,0:T(8,128)(2,1)S(1)} %shard_map.90), channel_id=1, replica_groups=mesh['y'=8,'c'=2,'z'=8,'x'=4] {'y','c'}, dimensions={0} | all-to-all | bytes 442368 | tf_op jit(solution)/shard_map/all_to_all | solution.py:297
  236.4 0.0 copy-done.3
  236.4 0.0 copy-done.5
  236.4 1.5 shard_map.91
  (11 shorter events, 0.1 us)
Async XLA Ops:
  7.2 93.6 %all-gather.3.cloned.1.call-start = ((), (), s32[]{:S(2)}) async-start(), calls=%async_computation.8 | async-start | bytes 3538944 | tf_op jit(solution)/shard_map/all_gather | solution.py:238
  7.2 0.7 copy-start
  7.9 0.7 copy-start.1
  8.7 0.7 copy-start.2
  9.4 0.7 copy-start.4
  45.6 121.5 %reduce-scatter.3.cloned.1.call-start = ((), (), s32[]{:S(2)}) async-start(), calls=%async_computation.9 | async-start | bytes 3538944 | tf_op jit(solution)/shard_map/reduce_scatter | solution.py:262
  75.6 32.6 %copy-start.6 = (bf16[768,640]{1,0:T(8,128)(2,1)}, bf16[768,640]{1,0:T(8,128)(2,1)S(1)}, u32[]{:S(2)}) copy-start(bf16[768,640]{1,0:T(8,128)(2,1)S(1)} %all-gather) | copy-start | bytes 2949124
  75.6 20.2 %collective-permute-start = (bf16[8,96,640]{2,1,0:T(8,128)(2,1)S(1)}, bf16[8,96,640]{2,1,0:T(8,128)(2,1)S(1)}, u32[]{:S(2)}, u32[]{:S(2)}) collective-permute-start(bf16[8,96,640]{2,1,0:T(8,128)(2,1)S(1)} %bitcast.17), channel_id=1, source_target_pairs={{0,1},{1,2},{2,3},{3,0},{4,5},{5,6},{6,7},{7,4},{8,9},{9,10},{10,1... | collective-permute-start | bytes 2949128 | tf_op jit(solution)/shard_map/ppermute | solution.py:240
  78.7 18.9 %collective-permute-start.1 = (bf16[8,96,640]{2,1,0:T(8,128)(2,1)S(1)}, bf16[8,96,640]{2,1,0:T(8,128)(2,1)S(1)}, u32[]{:S(2)}, u32[]{:S(2)}) collective-permute-start(bf16[8,96,640]{2,1,0:T(8,128)(2,1)S(1)} %bitcast.18), channel_id=1, source_target_pairs={{1,0},{2,1},{3,2},{0,3},{5,4},{6,5},{7,6},{4,7},{9,8},{10,9},{11,1... | collective-permute-start | bytes 2949128 | tf_op jit(solution)/shard_map/ppermute | solution.py:241
  95.8 12.5 %copy-start.7 = (bf16[8,96,640]{2,1,0:T(8,128)(2,1)}, bf16[8,96,640]{2,1,0:T(8,128)(2,1)S(1)}, u32[]{:S(2)}) copy-start(bf16[8,96,640]{2,1,0:T(8,128)(2,1)S(1)} %collective-permute-done.left) | copy-start | bytes 2949124
  97.7 14.3 %copy-start.8 = (bf16[8,96,640]{2,1,0:T(8,128)(2,1)}, bf16[8,96,640]{2,1,0:T(8,128)(2,1)S(1)}, u32[]{:S(2)}) copy-start(bf16[8,96,640]{2,1,0:T(8,128)(2,1)S(1)} %collective-permute-done.1.right) | copy-start | bytes 2949124
  108.2 91.1 %reduce-scatter.5.cloned.1.call-start = ((), (), s32[]{:S(2)}) async-start(), calls=%async_computation.10 | async-start | bytes 2654208 | tf_op jit(solution)/shard_map/reduce_scatter | solution.py:288
  109.1 11.6 %collective-permute-start.2 = (bf16[4,96,640]{2,1,0:T(8,128)(2,1)}, bf16[4,96,640]{2,1,0:T(8,128)(2,1)S(1)}, u32[]{:S(2)}, u32[]{:S(2)}) collective-permute-start(bf16[4,96,640]{2,1,0:T(8,128)(2,1)} %slice.6), channel_id=1, source_target_pairs={{0,1},{1,2},{2,3},{3,0},{4,5},{5,6},{6,7},{7,4},{8,9},{9,10},{10,1... | collective-permute-start | bytes 1474568 | tf_op jit(solution)/shard_map/ppermute | solution.py:260
  112.0 10.5 %collective-permute-start.3 = (bf16[4,96,640]{2,1,0:T(8,128)(2,1)S(1)}, bf16[4,96,640]{2,1,0:T(8,128)(2,1)S(1)}, u32[]{:S(2)}, u32[]{:S(2)}) collective-permute-start(bf16[4,96,640]{2,1,0:T(8,128)(2,1)S(1)} %slice.7), channel_id=1, source_target_pairs={{1,0},{2,1},{3,2},{0,3},{5,4},{6,5},{7,6},{4,7},{9,8},{10,9},{11,1... | collective-permute-start | bytes 1474568 | tf_op jit(solution)/shard_map/ppermute | solution.py:261
  120.8 1.8 copy-start.10
  122.6 0.8 copy-start.11
  133.6 1.4 copy-start.9
  167.1 69.3 %copy-start.3 = (s32[128,4]{0,1:T(4,128)S(1)}, s32[128,4]{0,1:T(4,128)}, u32[]{:S(2)}) copy-start(s32[128,4]{0,1:T(4,128)} %param.8) | copy-start | bytes 6148
  167.1 69.3 %copy-start.5 = (s32[128,4]{0,1:T(4,128)S(1)}, s32[128,4]{0,1:T(4,128)}, u32[]{:S(2)}) copy-start(s32[128,4]{0,1:T(4,128)} %param.9) | copy-start | bytes 6148
  167.1 32.2 %all-to-all-start.1 = ((bf16[4,96,512]{2,1,0:T(8,128)(2,1)}), bf16[4,96,512]{2,1,0:T(8,128)(2,1)S(1)}, u32[]{:S(2)}, u32[]{:S(2)}) async-start(bf16[4,96,512]{2,1,0:T(8,128)(2,1)} %bitcast.20), calls=%async_computation.2 | async-start | bytes 786432 | tf_op jit(solution)/shard_map/all_to_all | solution.py:292
Sparse Core Ops, SparseCore 0:
  45.8 54.9 all-gather.2
  108.4 44.4 reduce-scatter.2
  155.7 43.5 reduce-scatter.4

commit v3 on v2

v3 whole, which is shorter than its diff:
```python
import jax
import jax.numpy as jnp
from jax import lax
from jax.experimental import pallas as pl
from jax.experimental.pallas import tpu as pltpu
from jax.sharding import Mesh
from jax.sharding import PartitionSpec as P

EXPERTS = 16
CAP = 36
TOKENS_HERE = 128
FEATURES = 96
ROWS = EXPERTS * CAP
MAIN = 512
TAIL = ROWS - MAIN
WIDE = MAIN + 2 * TAIL
PLANES = 8
STEP = 4 * FEATURES
DEPTH = PLANES * STEP
EP = ("y", "c")
ETP = ("z", "x")
RIGHT = [(0, 1), (1, 2), (2, 3), (3, 0)]
LEFT = [(1, 0), (2, 1), (3, 2), (0, 3)]
NT = (((1,), (1,)), ((), ()))
TN = (((0,), (0,)), ((), ()))
NN = (((1,), (0,)), ((), ()))


def f32_dot(a, b, dims):
    return lax.dot_general(a, b, dims, preferred_element_type=jnp.float32)


def slots(routes, gate_fixed):
    named = []
    gates = []
    for e in range(EXPERTS):
        hit = routes == e
        named.append(jnp.sum(hit.astype(jnp.float32), axis=0, keepdims=True))
        gates.append(jnp.sum(jnp.where(hit, gate_fixed, 0).astype(jnp.float32), axis=0, keepdims=True))
    member = jnp.concatenate(named, axis=0)
    before = lax.broadcasted_iota(jnp.int32, (TOKENS_HERE, TOKENS_HERE), 0)
    after = lax.broadcasted_iota(jnp.int32, (TOKENS_HERE, TOKENS_HERE), 1)
    earlier = (before < after).astype(jnp.bfloat16)
    rank = jnp.dot(member.astype(jnp.bfloat16), earlier, preferred_element_type=jnp.float32)
    rank = jnp.where(member > 0.0, rank, -1.0)
    slot = lax.broadcasted_iota(jnp.int32, (CAP, TOKENS_HERE), 0).astype(jnp.float32)
    onehot = [(rank[e : e + 1] == slot).astype(jnp.float32) for e in range(EXPERTS)]
    return onehot, gates


def dispatch_body(routes_ref, gate_ref, tokens_ref, cot_ref, out_ref):
    onehot, gates = slots(routes_ref[...], gate_ref[...])
    values = jnp.concatenate([tokens_ref[...], cot_ref[...]], axis=0)
    is_token = lax.broadcasted_iota(jnp.int32, (CAP, 2 * FEATURES), 1) < FEATURES
    for e in range(EXPERTS):
        scale = jnp.sum(onehot[e] * gates[e], axis=1, keepdims=True) * (1.0 / 65536.0)
        rows = f32_dot(onehot[e].astype(jnp.bfloat16), values, NT)
        out_ref[e] = (rows * jnp.where(is_token, 1.0, scale)).astype(jnp.bfloat16)


def place_of(source):
    slot = lax.broadcasted_iota(jnp.int32, (CAP, MAIN + 2 * TAIL), 0)
    number = lax.broadcasted_iota(jnp.int32, (CAP, MAIN + 2 * TAIL), 1)
    return (number == slot + source * CAP).astype(jnp.bfloat16)


def columns_body(rows_ref, first_ref, second_ref):
    total = jnp.zeros((2 * FEATURES, WIDE), jnp.float32)
    for source in range(EXPERTS):
        total = total + f32_dot(rows_ref[source], place_of(source), TN)
    tokens, cotangent = total[:FEATURES], total[FEATURES:]
    first_ref[:, pl.ds(0, MAIN)] = tokens[:, :MAIN].astype(jnp.bfloat16)
    low = lax.broadcasted_iota(jnp.int32, (FEATURES, 2 * TAIL), 1) < TAIL
    tail = jnp.where(low, tokens[:, MAIN:], pltpu.roll(cotangent[:, MAIN:], TAIL, 1))
    first_ref[:, pl.ds(MAIN, 2 * TAIL)] = tail.astype(jnp.bfloat16)
    second_ref[...] = cotangent[:, :MAIN].astype(jnp.bfloat16)


def total_of(ref):
    total = ref[0].astype(jnp.float32)
    for k in range(1, ref.shape[0]):
        total = total + ref[k].astype(jnp.float32)
    return total


def rows_body(first_ref, second_ref, out_ref):
    first = total_of(first_ref)
    second = total_of(second_ref)
    tail = second[:, MAIN:]
    low = lax.broadcasted_iota(jnp.int32, tail.shape, 1) < TAIL
    outs = jnp.concatenate([first, jnp.where(low, tail, 0.0)], axis=1)
    grads = jnp.concatenate([second[:, :MAIN], jnp.where(low, pltpu.roll(tail, TAIL, 1), 0.0)], axis=1)
    both = jnp.concatenate([outs, grads], axis=0).astype(jnp.bfloat16)
    for source in range(EXPERTS):
        out_ref[source] = f32_dot(place_of(source), both, NT).astype(jnp.bfloat16)


def combine_body(routes_ref, gate_ref, rows_ref, out_ref, grad_ref):
    onehot, gates = slots(routes_ref[...], gate_ref[...])
    total = jnp.zeros((2 * FEATURES, 3 * TOKENS_HERE), jnp.float32)
    for e in range(EXPERTS):
        high = jnp.floor(gates[e] * (1.0 / 256.0))
        low = gates[e] - 256.0 * high
        factors = jnp.concatenate([onehot[e] * high, onehot[e] * low, onehot[e]], axis=1).astype(jnp.bfloat16)
        total = total + f32_dot(rows_ref[e], factors, TN)
    by_high, by_low = total[:FEATURES, :TOKENS_HERE], total[:FEATURES, TOKENS_HERE : 2 * TOKENS_HERE]
    out_ref[...] = (by_high * (1.0 / 256.0) + by_low * (1.0 / 65536.0)).astype(jnp.bfloat16)
    grad_ref[...] = total[FEATURES:, 2 * TOKENS_HERE :].astype(jnp.bfloat16)


def activation(pre_gate, pre_up):
    sig = jax.nn.sigmoid(pre_gate)
    activated = pre_gate * sig
    derivative = sig * (1.0 + pre_gate * (1.0 - sig))
    return activated * pre_up, pre_up * derivative, activated


def start_all(copies):
    for copy in copies:
        copy.start()


def wait_all(copies):
    for copy in copies:
        copy.wait()


def expert_body(
    x_index,
    first_ref,
    own,
    left,
    right,
    far_low,
    far_high,
    gate_ref,
    up_ref,
    down_ref,
    y_first_ref,
    y_second_ref,
    first,
    second,
    gate,
    up,
    down,
    y_first,
    y_second,
    sems,
    first_sems,
    second_sems,
):
    me = x_index[0]
    whole, low, high = pl.ds(0, 8), pl.ds(0, 4), pl.ds(4, 4)
    pieces = ((own, whole, 0), (left, whole, 3), (right, whole, 1), (far_low, low, 2), (far_high, high, 2))
    loads = [
        pltpu.make_async_copy(source, target, sems.at[number])
        for number, (source, target) in enumerate(((first_ref, first), (gate_ref, gate), (up_ref, up), (down_ref, down)))
    ]
    for number, (source, planes, away) in enumerate(pieces):
        target = second.at[planes, lax.rem(me + away, 4)]
        loads.append(pltpu.make_async_copy(source, target, sems.at[4 + number]))
    start_all(loads)
    wait_all(loads[:2])
    pre_gate = f32_dot(gate[0], first[...], NN)
    loads[2].wait()
    pre_up = f32_dot(up[0], first[...], NN)
    hidden, to_gate, to_up = activation(pre_gate, pre_up)
    wait_all(loads[3:])
    grad_hidden = f32_dot(down[0], second[...].reshape(DEPTH, MAIN), NN)
    tail_grad = f32_dot(down[0], first[:, pl.ds(MAIN, 2 * TAIL)], NN)
    is_low = lax.broadcasted_iota(jnp.int32, tail_grad.shape, 1) < TAIL
    tail_hidden = jnp.where(is_low, hidden[:, MAIN:], 0.0).astype(jnp.bfloat16)
    tail_gate = jnp.where(is_low, 0.0, tail_grad * pltpu.roll(to_gate[:, MAIN:], TAIL, 1)).astype(jnp.bfloat16)
    tail_up = jnp.where(is_low, 0.0, tail_grad * pltpu.roll(to_up[:, MAIN:], TAIL, 1)).astype(jnp.bfloat16)
    grad_gate = jnp.concatenate([(grad_hidden * to_gate[:, :MAIN]).astype(jnp.bfloat16), tail_gate], axis=1)
    grad_up = jnp.concatenate([(grad_hidden * to_up[:, :MAIN]).astype(jnp.bfloat16), tail_up], axis=1)
    hidden = jnp.concatenate([hidden[:, :MAIN].astype(jnp.bfloat16), tail_hidden], axis=1)
    stores = []
    for step in range(PLANES):
        part = pl.ds(step * STEP, STEP)
        out = f32_dot(down[0, :, part], hidden, TN)
        value = f32_dot(gate[0, :, part], grad_gate, TN) + f32_dot(up[0, :, part], grad_up, TN)
        y_first[:, step] = out[:, :MAIN].astype(jnp.bfloat16).reshape(4, FEATURES, MAIN)
        y_second[step, :, pl.ds(0, MAIN)] = value[:, :MAIN].astype(jnp.bfloat16)
        y_second[step, :, pl.ds(MAIN, 2 * TAIL)] = (value[:, MAIN:] + out[:, MAIN:]).astype(jnp.bfloat16)
        stores.append(pltpu.make_async_copy(y_first.at[:, step], y_first_ref.at[:, step], first_sems.at[step]))
        stores.append(pltpu.make_async_copy(y_second.at[step], y_second_ref.at[step], second_sems.at[step]))
        start_all(stores[-2:])
    wait_all(stores)


def call(body, outs, *args, specs=None, out_specs=None, scratch=(), limit=24):
    vmem = pl.BlockSpec(memory_space=pltpu.VMEM)
    return pl.pallas_call(
        body,
        out_shape=outs,
        in_specs=specs or [vmem] * len(args),
        out_specs=out_specs or jax.tree.map(lambda _: vmem, outs),
        scratch_shapes=scratch,
        compiler_params=pltpu.CompilerParams(vmem_limit_bytes=limit * 2**20),
    )(*args)


def bf16(*shape):
    return jax.ShapeDtypeStruct(shape, jnp.bfloat16)


def shards(tokens, routes, gate_fixed, gate_weight, up_weight, down_weight, cotangent):
    named = (routes.T, gate_fixed.T)
    weights = (gate_weight, up_weight, down_weight)
    send = call(dispatch_body, bf16(EXPERTS, CAP, 2 * FEATURES), *named, tokens.T, cotangent.T, limit=56)
    received = lax.all_to_all(send, EP, 0, 0, tiled=True)
    first, second = call(columns_body, (bf16(FEATURES, WIDE), bf16(FEATURES, MAIN)), received)

    first = lax.all_gather(first, "x", axis=0, tiled=True)
    first, second = lax.optimization_barrier((first, second))
    first = lax.all_gather(first, "z", axis=0, tiled=True)
    own = lax.all_gather(second, "z", axis=0, tiled=False)
    left = lax.ppermute(own, "x", RIGHT)
    right = lax.ppermute(own, "x", LEFT)
    far_low = lax.ppermute(left[:4], "x", RIGHT)
    far_high = lax.ppermute(right[4:], "x", LEFT)

    hbm = pl.BlockSpec(memory_space=pltpu.HBM)
    weight = pltpu.VMEM(gate_weight.shape, jnp.bfloat16)
    outs = (bf16(4, PLANES, FEATURES, MAIN), bf16(PLANES, STEP, WIDE))
    y_first, y_second = call(
        expert_body,
        outs,
        lax.axis_index("x").astype(jnp.int32).reshape(1),
        first,
        own,
        left,
        right,
        far_low,
        far_high,
        *weights,
        specs=[pl.BlockSpec(memory_space=pltpu.SMEM)] + [hbm] * 9,
        out_specs=(hbm, hbm),
        scratch=[pltpu.VMEM((DEPTH, WIDE), jnp.bfloat16), pltpu.VMEM((PLANES, 4, FEATURES, MAIN), jnp.bfloat16)]
        + [weight] * 3
        + [pltpu.VMEM(out.shape, jnp.bfloat16) for out in outs]
        + [pltpu.SemaphoreType.DMA((9,)), pltpu.SemaphoreType.DMA((PLANES,)), pltpu.SemaphoreType.DMA((PLANES,))],
        limit=56,
    )
    y_second = lax.psum_scatter(y_second, "z", scatter_dimension=0, tiled=False)
    y_first = lax.all_to_all(y_first, "x", 0, 0, tiled=True)
    y_first = jnp.sum(y_first.astype(jnp.float32), axis=0).astype(jnp.bfloat16)
    y_first = lax.all_to_all(y_first, "z", 0, 0, tiled=True)
    y_first, y_second = lax.optimization_barrier((y_first, y_second))
    y_second = lax.all_to_all(y_second.reshape(4, FEATURES, WIDE), "x", 0, 0, tiled=True)

    back = call(rows_body, bf16(EXPERTS, CAP, 2 * FEATURES), y_first, y_second)
    home = lax.all_to_all(back, EP, 0, 0, tiled=True)
    out, grad = call(combine_body, (bf16(FEATURES, TOKENS_HERE), bf16(FEATURES, TOKENS_HERE)), *named, home)
    return out.T, grad.T


def solution(mesh):
    fine = Mesh(mesh.devices.reshape(8, 2, 8, 4), ("y", "c", "z", "x"))
    ep, etp = EP, ETP
    placed = (P(ep, etp), P(ep, None), P(ep, None), P(ep, etp, None), P(ep, etp, None), P(ep, etp, None), P(ep, etp))
    return jax.shard_map(shards, mesh=fine, in_specs=placed, out_specs=(P(ep, etp), P(ep, etp)), check_vma=False)
```

time: 245 us -> 237 us (0.967)
  blocking collectives: 131 us -> 162 us
  waiting for transfers between devices: 54.2 us -> 27.4 us
  local copies, waits for them, and re-layouts: 5.88 us -> 0.89 us
  Pallas kernels: 22.5 us -> 17.9 us
  starting transfers between devices: 16.7 us -> 12.9 us
    all_to_all x3, blocking collectives: 41.4 us -> 76.8 us  [the longest x1 32.4 us: shards(): y_first = lax.all_to_all(y_first, 'x', 0, 0, tiled=True)]
    reduce_scatter x1, waiting for transfers between devices: 28.6 us -> 8.95 us  [shards(): y_second = lax.psum_scatter(y_second, 'z', scatter_dimension=0, tiled=False)]
    ppermute x1, waiting for transfers between devices: 13.7 us -> 0.01 us  [shards(): left = lax.ppermute(own, 'x', RIGHT)]
    ppermute x1, waiting for transfers between devices: 1.87 us -> 8.91 us  [shards(): right = lax.ppermute(own, 'x', LEFT)]
    unnamed x24 -> x14, local copies, waits for them, and re-layouts: 5.01 us -> 0.03 us
    pallas_call x6 -> x5, Pallas kernels: 22.5 us -> 17.9 us  [call(): pl.pallas_call(body, out_shape=outs, in_specs=specs or [vmem] * len(args)...]
    all_to_all x1, blocking collectives: 25.9 us -> 21.5 us  [shards(): home = lax.all_to_all(back, EP, 0, 0, tiled=True)]
    all_to_all x1 -> x0, starting transfers between devices: 3.59 us -> none  [shards(): lax.all_to_all(y_first.reshape(4, FEATURES, MAIN), 'x', 0, 0, tiled=True)]
  transfers between devices with their start and end apart: 8 -> 6, of which waited for: 6 -> 5; matrix products, arithmetic and copies ran while one was open for 0% -> 1% of each run, Pallas kernels for 4% -> 0%
where the time goes in v3:
time: 237 us
  blocking collectives  162 us (68%)
  waiting for transfers between devices  27.4 us (12%)
  Pallas kernels  17.9 us (8%)
  between operations  14.1 us (6%)
  starting transfers between devices  12.9 us (5%)
    all_to_all x1, blocking collectives, shards(): y_first = lax.all_to_all(y_first, 'x', 0, 0, tiled=True)  32.4 us
    all_to_all x1, blocking collectives, shards(): y_first = lax.all_to_all(y_first, 'z', 0, 0, tiled=True)  31.8 us
    all_gather x1, blocking collectives, shards(): own = lax.all_gather(second, 'z', axis=0, tiled=False)  27.9 us
    all_to_all x1, blocking collectives, shards(): received = lax.all_to_all(send, EP, 0, 0, tiled=True)  23.2 us
    all_to_all x1, blocking collectives, shards(): home = lax.all_to_all(back, EP, 0, 0, tiled=True)  21.5 us
    pallas_call x5, Pallas kernels, call(): pl.pallas_call(body, out_shape=outs, in_specs=specs or [vmem] * len(args)...  17.9 us
    all_to_all x1, blocking collectives, shards(): lax.all_to_all(y_second.reshape(4, FEATURES, WIDE), 'x', 0, 0, tiled=True)  12.6 us
    all_gather x1, blocking collectives, shards(): first = lax.all_gather(first, 'x', axis=0, tiled=True)  12.3 us
  transfers between devices with their start and end apart: 6, of which 5 were waited for; matrix products, arithmetic and copies ran while one was open for 1% of the time, Pallas kernels for 0%

profile of v3, /device:TPU:1, one launch (start us, length us, event | category | flops | bytes accessed | tf_op | source)
XLA Modules:
  0.0 236.5 jit_solution(6443529871874134069)
XLA Ops:
  7.2 0.0 all-gather.3.cloned.1.call-start
  7.2 2.2 shard_map.86
  9.4 23.2 %all_to_all.25.rows_ref = bf16[16,36,192]{2,1,0:T(8,128)(2,1)S(1)} all-to-all(bf16[16,36,192]{2,1,0:T(8,128)(2,1)} %shard_map.86), channel_id=1, replica_groups=mesh['y'=8,'c'=2,'z'=8,'x'=4] {'y','c'}, dimensions={0} | all-to-all | bytes 442368 | tf_op jit(solution)/shard_map/all_to_all | solution.py:212
  32.7 1.0 shard_map.87
  33.7 12.3 %all_gather.12 = bf16[384,640]{1,0:T(8,128)(2,1)} all-gather(bf16[96,640]{1,0:T(8,128)(2,1)S(1)} %get-tuple-element.12), channel_id=1, replica_groups=mesh['y'=8,'c'=2,'z'=8,'x'=4] {'x'}, dimensions={0}, use_global_device_ids=true | all-gather | bytes 614400 | tf_op jit(solution)/shard_map/all_gather | solution.py:215
  46.0 0.0 all-gather.3.cloned.1.call-update
  46.0 0.0 reduce-scatter.2.cloned.1.call-start
  46.1 27.9 %all-gather = bf16[768,512]{1,0:T(8,128)(2,1)S(1)} all-gather(bf16[96,512]{1,0:T(8,128)(2,1)S(1)} %get-tuple-element.15), channel_id=2, replica_groups=mesh['y'=8,'c'=2,'z'=8,'x'=4] {'z'}, dimensions={0}, use_global_device_ids=true | all-gather | bytes 884736 | tf_op jit(solution)/shard_map/all_gather | solution.py:218
  73.9 0.0 copy-start.2
  73.9 4.0 %collective-permute-start.1 = (bf16[8,96,512]{2,1,0:T(8,128)(2,1)S(1)}, bf16[8,96,512]{2,1,0:T(8,128)(2,1)S(1)}, u32[]{:S(2)}, u32[]{:S(2)}) collective-permute-start(bf16[8,96,512]{2,1,0:T(8,128)(2,1)S(1)} %bitcast.14), channel_id=1, source_target_pairs={{1,0},{2,1},{3,2},{0,3},{5,4},{6,5},{7,6},{4,7},{9,8},{10,9},{11,1... | collective-permute-start | bytes 2359304 | tf_op jit(solution)/shard_map/ppermute | solution.py:220
  78.0 1.9 collective-permute-start
  79.9 8.9 %collective-permute-done.1.right = bf16[8,96,512]{2,1,0:T(8,128)(2,1)S(1)} collective-permute-done((bf16[8,96,512]{2,1,0:T(8,128)(2,1)S(1)}, bf16[8,96,512]{2,1,0:T(8,128)(2,1)S(1)}, u32[]{:S(2)}, u32[]{:S(2)}) %collective-permute-start.1) | collective-permute-done | bytes 786464 | tf_op jit(solution)/shard_map/ppermute | solution.py:220
  88.8 0.0 copy-start.3
  88.9 5.0 %collective-permute-start.3 = (bf16[4,96,512]{2,1,0:T(8,128)(2,1)S(1)}, bf16[4,96,512]{2,1,0:T(8,128)(2,1)S(1)}, u32[]{:S(2)}, u32[]{:S(2)}) collective-permute-start(bf16[4,96,512]{2,1,0:T(8,128)(2,1)S(1)} %slice.9), channel_id=1, source_target_pairs={{1,0},{2,1},{3,2},{0,3},{5,4},{6,5},{7,6},{4,7},{9,8},{10,9},{11,1... | collective-permute-start | bytes 1179656 | tf_op jit(solution)/shard_map/ppermute | solution.py:222
  93.8 0.0 collective-permute-done.left
  93.9 0.0 copy-start.4
  93.9 0.8 slice.8
  94.7 1.9 collective-permute-start.2
  96.6 3.1 %collective-permute-done.3.far_high = bf16[4,96,512]{2,1,0:T(8,128)(2,1)S(1)} collective-permute-done((bf16[4,96,512]{2,1,0:T(8,128)(2,1)S(1)}, bf16[4,96,512]{2,1,0:T(8,128)(2,1)S(1)}, u32[]{:S(2)}, u32[]{:S(2)}) %collective-permute-start.3) | collective-permute-done | bytes 393248 | tf_op jit(solution)/shard_map/ppermute | solution.py:222
  99.7 0.0 copy-start.5
  99.7 5.3 %collective-permute-done.2.far_low = bf16[4,96,512]{2,1,0:T(8,128)(2,1)S(1)} collective-permute-done((bf16[4,96,512]{2,1,0:T(8,128)(2,1)}, bf16[4,96,512]{2,1,0:T(8,128)(2,1)S(1)}, u32[]{:S(2)}, u32[]{:S(2)}) %collective-permute-start.2) | collective-permute-done | bytes 393248 | tf_op jit(solution)/shard_map/ppermute | solution.py:221
  105.0 0.0 copy-start.6
  105.0 1.1 all-gather.3.cloned.1.call-done.first_ref
  106.1 0.0 copy-done.2
  106.1 0.0 copy-done.3
  106.1 0.0 copy-done.4
  106.1 0.0 copy-done.5
  106.1 0.0 copy-done.6
  106.1 11.6 %shard_map.88 = (bf16[4,8,96,512]{3,2,1,0:T(8,128)(2,1)}, bf16[8,384,640]{2,1,0:T(8,128)(2,1)}) custom-call(s32[1]{0:T(128)} %bitcast.2.x_index, bf16[3072,640]{1,0:T(8,128)(2,1)} %all-gather.3.cloned.1.call-done.first_ref, bf16[8,96,512]{2,1,0:T(8,128)(2,1)} %bitcast.16, bf16[8,96,512]{2,1,0:T(8,128)(2,1)} %copy-done.4, bf16[8,96,512]{2,1,0:T(8,128)(2,1)} %copy-done.3, ...), custom_call_target="tpu_custom_call" | custom-call | tf_op jit(solution)/shard_map/pallas_call | solution.py:194
  117.7 0.0 reduce-scatter.2.cloned.1.call-update
  117.7 32.4 %all_to_all.26 = bf16[4,8,96,512]{3,2,1,0:T(8,128)(2,1)S(1)} all-to-all(bf16[4,8,96,512]{3,2,1,0:T(8,128)(2,1)} %get-tuple-element.16), channel_id=1, replica_groups=mesh['y'=8,'c'=2,'z'=8,'x'=4] {'x'}, dimensions={0} | all-to-all | bytes 6291456 | tf_op jit(solution)/shard_map/all_to_all | solution.py:247
  150.2 1.6 reduce_sum.12
  151.8 0.0 copy-start
  151.8 0.0 copy-start.1
  151.8 31.8 %all_to_all.27.first_ref = bf16[8,96,512]{2,1,0:T(8,128)(2,1)S(1)} all-to-all(bf16[8,96,512]{2,1,0:T(8,128)(2,1)} %reduce_sum.12), channel_id=1, replica_groups=mesh['y'=8,'c'=2,'z'=8,'x'=4] {'z'}, dimensions={0} | all-to-all | bytes 1572864 | tf_op jit(solution)/shard_map/all_to_all | solution.py:249
  183.6 9.0 %reduce-scatter.2.cloned.1.call-done = bf16[1,384,640]{2,1,0:T(8,128)(2,1)} async-done(((bf16[8,384,640]{2,1,0:T(8,128)(2,1)}), bf16[1,384,640]{2,1,0:T(8,128)(2,1)}) %reduce-scatter.2.cloned.1.call-update) | async-done | bytes 491536 | tf_op jit(solution)/shard_map/reduce_scatter | solution.py:246
  192.6 12.6 %all_to_all.28.second_ref = bf16[4,96,640]{2,1,0:T(8,128)(2,1)S(1)} all-to-all(bf16[4,96,640]{2,1,0:T(8,128)(2,1)} %bitcast.17), channel_id=1, replica_groups=mesh['y'=8,'c'=2,'z'=8,'x'=4] {'x'}, dimensions={0} | all-to-all | bytes 983040 | tf_op jit(solution)/shard_map/all_to_all | solution.py:251
  205.1 1.6 shard_map.89
  206.7 21.5 %all_to_all.29.rows_ref = bf16[16,36,192]{2,1,0:T(8,128)(2,1)S(1)} all-to-all(bf16[16,36,192]{2,1,0:T(8,128)(2,1)S(1)} %shard_map.89), channel_id=1, replica_groups=mesh['y'=8,'c'=2,'z'=8,'x'=4] {'y','c'}, dimensions={0} | all-to-all | bytes 442368 | tf_op jit(solution)/shard_map/all_to_all | solution.py:254
  228.2 0.0 copy-done
  228.2 0.0 copy-done.1
  228.2 1.5 shard_map.90
  (1 shorter events, 0.0 us)
Async XLA Ops:
  7.2 99.0 %all-gather.3.cloned.1.call-start = ((), (), s32[]{:S(2)}) async-start(), calls=%async_computation.6 | async-start | bytes 4423680 | tf_op jit(solution)/shard_map/all_gather | solution.py:217
  46.0 146.5 %reduce-scatter.2.cloned.1.call-start = ((), (), s32[]{:S(2)}) async-start(), calls=%async_computation.7 | async-start | bytes 4423680 | tf_op jit(solution)/shard_map/reduce_scatter | solution.py:246
  73.9 32.2 %copy-start.2 = (bf16[768,512]{1,0:T(8,128)(2,1)}, bf16[768,512]{1,0:T(8,128)(2,1)S(1)}, u32[]{:S(2)}) copy-start(bf16[768,512]{1,0:T(8,128)(2,1)S(1)} %all-gather) | copy-start | bytes 2359300
  73.9 14.9 %collective-permute-start.1 = (bf16[8,96,512]{2,1,0:T(8,128)(2,1)S(1)}, bf16[8,96,512]{2,1,0:T(8,128)(2,1)S(1)}, u32[]{:S(2)}, u32[]{:S(2)}) collective-permute-start(bf16[8,96,512]{2,1,0:T(8,128)(2,1)S(1)} %bitcast.14), channel_id=1, source_target_pairs={{1,0},{2,1},{3,2},{0,3},{5,4},{6,5},{7,6},{4,7},{9,8},{10,9},{11,1... | collective-permute-start | bytes 2359304 | tf_op jit(solution)/shard_map/ppermute | solution.py:220
  78.0 15.9 %collective-permute-start = (bf16[8,96,512]{2,1,0:T(8,128)(2,1)S(1)}, bf16[8,96,512]{2,1,0:T(8,128)(2,1)S(1)}, u32[]{:S(2)}, u32[]{:S(2)}) collective-permute-start(bf16[8,96,512]{2,1,0:T(8,128)(2,1)S(1)} %bitcast.15), channel_id=1, source_target_pairs={{0,1},{1,2},{2,3},{3,0},{4,5},{5,6},{6,7},{7,4},{8,9},{9,10},{10,1... | collective-permute-start | bytes 2359304 | tf_op jit(solution)/shard_map/ppermute | solution.py:219
  88.8 17.3 %copy-start.3 = (bf16[8,96,512]{2,1,0:T(8,128)(2,1)}, bf16[8,96,512]{2,1,0:T(8,128)(2,1)S(1)}, u32[]{:S(2)}) copy-start(bf16[8,96,512]{2,1,0:T(8,128)(2,1)S(1)} %collective-permute-done.1.right) | copy-start | bytes 2359300
  88.9 10.9 %collective-permute-start.3 = (bf16[4,96,512]{2,1,0:T(8,128)(2,1)S(1)}, bf16[4,96,512]{2,1,0:T(8,128)(2,1)S(1)}, u32[]{:S(2)}, u32[]{:S(2)}) collective-permute-start(bf16[4,96,512]{2,1,0:T(8,128)(2,1)S(1)} %slice.9), channel_id=1, source_target_pairs={{1,0},{2,1},{3,2},{0,3},{5,4},{6,5},{7,6},{4,7},{9,8},{10,9},{11,1... | collective-permute-start | bytes 1179656 | tf_op jit(solution)/shard_map/ppermute | solution.py:222
  93.9 12.3 %copy-start.4 = (bf16[8,96,512]{2,1,0:T(8,128)(2,1)}, bf16[8,96,512]{2,1,0:T(8,128)(2,1)S(1)}, u32[]{:S(2)}) copy-start(bf16[8,96,512]{2,1,0:T(8,128)(2,1)S(1)} %collective-permute-done.left) | copy-start | bytes 2359300
  94.7 10.3 %collective-permute-start.2 = (bf16[4,96,512]{2,1,0:T(8,128)(2,1)}, bf16[4,96,512]{2,1,0:T(8,128)(2,1)S(1)}, u32[]{:S(2)}, u32[]{:S(2)}) collective-permute-start(bf16[4,96,512]{2,1,0:T(8,128)(2,1)} %slice.8), channel_id=1, source_target_pairs={{0,1},{1,2},{2,3},{3,0},{4,5},{5,6},{6,7},{7,4},{8,9},{9,10},{10,1... | collective-permute-start | bytes 1179656 | tf_op jit(solution)/shard_map/ppermute | solution.py:221
  99.7 6.4 %copy-start.5 = (bf16[4,96,512]{2,1,0:T(8,128)(2,1)}, bf16[4,96,512]{2,1,0:T(8,128)(2,1)S(1)}, u32[]{:S(2)}) copy-start(bf16[4,96,512]{2,1,0:T(8,128)(2,1)S(1)} %collective-permute-done.3.far_high) | copy-start | bytes 1179652
  105.0 1.1 copy-start.6
  151.8 76.4 %copy-start = (s32[128,4]{0,1:T(4,128)S(1)}, s32[128,4]{0,1:T(4,128)}, u32[]{:S(2)}) copy-start(s32[128,4]{0,1:T(4,128)} %param.8) | copy-start | bytes 6148
  151.8 76.4 %copy-start.1 = (s32[128,4]{0,1:T(4,128)S(1)}, s32[128,4]{0,1:T(4,128)}, u32[]{:S(2)}) copy-start(s32[128,4]{0,1:T(4,128)} %param.9) | copy-start | bytes 6148
Sparse Core Ops, SparseCore 0:
  46.2 59.9 all-gather.2
  117.8 74.6 reduce-scatter.1

commit v4 on v3

--- a/solution.py
+++ b/solution.py
@@ -129,8 +129,10 @@
     x_index,
     first_ref,
     own,
-    left,
-    right,
+    left_low,
+    left_high,
+    right_low,
+    right_high,
     far_low,
     far_high,
     gate_ref,
@@ -151,7 +153,15 @@
 ):
     me = x_index[0]
     whole, low, high = pl.ds(0, 8), pl.ds(0, 4), pl.ds(4, 4)
-    pieces = ((own, whole, 0), (left, whole, 3), (right, whole, 1), (far_low, low, 2), (far_high, high, 2))
+    pieces = (
+        (own, whole, 0),
+        (left_low, low, 3),
+        (left_high, high, 3),
+        (right_low, low, 1),
+        (right_high, high, 1),
+        (far_low, low, 2),
+        (far_high, high, 2),
+    )
     loads = [
         pltpu.make_async_copy(source, target, sems.at[number])
         for number, (source, target) in enumerate(((first_ref, first), (gate_ref, gate), (up_ref, up), (down_ref, down)))
@@ -216,10 +226,12 @@
     first, second = lax.optimization_barrier((first, second))
     first = lax.all_gather(first, "z", axis=0, tiled=True)
     own = lax.all_gather(second, "z", axis=0, tiled=False)
-    left = lax.ppermute(own, "x", RIGHT)
-    right = lax.ppermute(own, "x", LEFT)
-    far_low = lax.ppermute(left[:4], "x", RIGHT)
-    far_high = lax.ppermute(right[4:], "x", LEFT)
+    left_low = lax.ppermute(own[:4], "x", RIGHT)
+    right_high = lax.ppermute(own[4:], "x", LEFT)
+    left_high = lax.ppermute(own[4:], "x", RIGHT)
+    right_low = lax.ppermute(own[:4], "x", LEFT)
+    far_low = lax.ppermute(left_low, "x", RIGHT)
+    far_high = lax.ppermute(right_high, "x", LEFT)
 
     hbm = pl.BlockSpec(memory_space=pltpu.HBM)
     weight = pltpu.VMEM(gate_weight.shape, jnp.bfloat16)
@@ -230,17 +242,19 @@
         lax.axis_index("x").astype(jnp.int32).reshape(1),
         first,
         own,
-        left,
-        right,
+        left_low,
+        left_high,
+        right_low,
+        right_high,
         far_low,
         far_high,
         *weights,
-        specs=[pl.BlockSpec(memory_space=pltpu.SMEM)] + [hbm] * 9,
+        specs=[pl.BlockSpec(memory_space=pltpu.SMEM)] + [hbm] * 11,
         out_specs=(hbm, hbm),
         scratch=[pltpu.VMEM((DEPTH, WIDE), jnp.bfloat16), pltpu.VMEM((PLANES, 4, FEATURES, MAIN), jnp.bfloat16)]
         + [weight] * 3
         + [pltpu.VMEM(out.shape, jnp.bfloat16) for out in outs]
-        + [pltpu.SemaphoreType.DMA((9,)), pltpu.SemaphoreType.DMA((PLANES,)), pltpu.SemaphoreType.DMA((PLANES,))],
+        + [pltpu.SemaphoreType.DMA((11,)), pltpu.SemaphoreType.DMA((PLANES,)), pltpu.SemaphoreType.DMA((PLANES,))],
         limit=56,
     )
     y_second = lax.psum_scatter(y_second, "z", scatter_dimension=0, tiled=False)

time: 237 us -> 233 us (0.983)
  waiting for transfers between devices: 27.4 us -> 13 us
  starting transfers between devices: 12.9 us -> 18.3 us
  blocking collectives: 162 us -> 166 us
    reduce_scatter x1, waiting for transfers between devices: 8.95 us -> 0.01 us  [shards(): y_second = lax.psum_scatter(y_second, 'z', scatter_dimension=0, tiled=False)]
    ppermute x4 -> x6, waiting for transfers between devices: 17.3 us -> 9.38 us  [the longest x1 6.54 us: shards(): far_low = lax.ppermute(left_low, 'x', RIGHT)]
    ppermute x4 -> x6, starting transfers between devices: 12.8 us -> 18.3 us  [the longest x1 4.57 us: shards(): far_high = lax.ppermute(right_high, 'x', LEFT)]
    all_to_all x1, blocking collectives: 32.4 us -> 37.6 us  [shards(): y_first = lax.all_to_all(y_first, 'x', 0, 0, tiled=True)]
    all_to_all x1, blocking collectives: 21.5 us -> 24.7 us  [shards(): home = lax.all_to_all(back, EP, 0, 0, tiled=True)]
    all_gather x1, waiting for transfers between devices: 1.09 us -> 3.57 us  [shards(): first = lax.all_gather(first, 'z', axis=0, tiled=True)]
    all_to_all x1, blocking collectives: 31.8 us -> 29.3 us  [shards(): y_first = lax.all_to_all(y_first, 'z', 0, 0, tiled=True)]
  transfers between devices with their start and end apart: 6 -> 8, of which waited for: 5 -> 3; matrix products, arithmetic and copies ran while one was open for 1% -> 1% of each run, Pallas kernels for 0% -> 0%
where the time goes in v4:
time: 233 us; the launch traced here: 232 us
  blocking collectives  166 us (71%)
  starting transfers between devices  18.3 us (8%)
  Pallas kernels  17.9 us (8%)
  between operations  14.2 us (6%)
  waiting for transfers between devices  13 us (6%)
    all_to_all x1, blocking collectives, shards(): y_first = lax.all_to_all(y_first, 'x', 0, 0, tiled=True)  37.6 us
    all_to_all x1, blocking collectives, shards(): y_first = lax.all_to_all(y_first, 'z', 0, 0, tiled=True)  29.3 us
    all_gather x1, blocking collectives, shards(): own = lax.all_gather(second, 'z', axis=0, tiled=False)  27.8 us
    all_to_all x1, blocking collectives, shards(): home = lax.all_to_all(back, EP, 0, 0, tiled=True)  24.7 us
    all_to_all x1, blocking collectives, shards(): received = lax.all_to_all(send, EP, 0, 0, tiled=True)  23.2 us
    pallas_call x5, Pallas kernels, call(): pl.pallas_call(body, out_shape=outs, in_specs=specs or [vmem] * len(args)...  17.9 us
    all_gather x1, blocking collectives, shards(): first = lax.all_gather(first, 'x', axis=0, tiled=True)  12.3 us
    all_to_all x1, blocking collectives, shards(): lax.all_to_all(y_second.reshape(4, FEATURES, WIDE), 'x', 0, 0, tiled=True)  11 us
  transfers between devices with their start and end apart: 8, of which 3 were waited for; matrix products, arithmetic and copies ran while one was open for 1% of the time, Pallas kernels for 0%

profile of v4, /device:TPU:1, one launch (start us, length us, event | category | flops | bytes accessed | tf_op | source)
XLA Modules:
  0.0 231.9 jit_solution(17411458435883943130)
XLA Ops:
  7.2 0.0 all-gather.3.cloned.1.call-start
  7.2 2.2 shard_map.86
  9.4 23.2 %all_to_all.25.rows_ref = bf16[16,36,192]{2,1,0:T(8,128)(2,1)S(1)} all-to-all(bf16[16,36,192]{2,1,0:T(8,128)(2,1)} %shard_map.86), channel_id=1, replica_groups=mesh['y'=8,'c'=2,'z'=8,'x'=4] {'y','c'}, dimensions={0} | all-to-all | bytes 442368 | tf_op jit(solution)/shard_map/all_to_all | solution.py:222
  32.7 1.0 shard_map.87
  33.7 12.3 %all_gather.12 = bf16[384,640]{1,0:T(8,128)(2,1)} all-gather(bf16[96,640]{1,0:T(8,128)(2,1)S(1)} %get-tuple-element.12), channel_id=1, replica_groups=mesh['y'=8,'c'=2,'z'=8,'x'=4] {'x'}, dimensions={0}, use_global_device_ids=true | all-gather | bytes 614400 | tf_op jit(solution)/shard_map/all_gather | solution.py:225
  46.0 0.0 all-gather.3.cloned.1.call-update
  46.0 0.0 reduce-scatter.2.cloned.1.call-start
  46.1 27.8 %all-gather = bf16[768,512]{1,0:T(8,128)(2,1)S(1)} all-gather(bf16[96,512]{1,0:T(8,128)(2,1)S(1)} %get-tuple-element.15), channel_id=2, replica_groups=mesh['y'=8,'c'=2,'z'=8,'x'=4] {'z'}, dimensions={0}, use_global_device_ids=true | all-gather | bytes 884736 | tf_op jit(solution)/shard_map/all_gather | solution.py:228
  73.9 0.0 copy-start.2
  73.9 0.9 fusion
  74.8 2.9 %collective-permute-start = (bf16[4,96,512]{2,1,0:T(8,128)(2,1)}, bf16[4,96,512]{2,1,0:T(8,128)(2,1)S(1)}, u32[]{:S(2)}, u32[]{:S(2)}) collective-permute-start(bf16[4,96,512]{2,1,0:T(8,128)(2,1)} %bitcast.6), channel_id=1, source_target_pairs={{0,1},{1,2},{2,3},{3,0},{4,5},{5,6},{6,7},{7,4},{8,9},{9,10},{10,1... | collective-permute-start | bytes 1179656 | tf_op jit(solution)/shard_map/ppermute | solution.py:229
  77.7 3.6 %collective-permute-start.3 = (bf16[4,96,512]{2,1,0:T(8,128)(2,1)S(1)}, bf16[4,96,512]{2,1,0:T(8,128)(2,1)S(1)}, u32[]{:S(2)}, u32[]{:S(2)}) collective-permute-start(bf16[4,96,512]{2,1,0:T(8,128)(2,1)S(1)} %bitcast.18), channel_id=1, source_target_pairs={{1,0},{2,1},{3,2},{0,3},{5,4},{6,5},{7,6},{4,7},{9,8},{10,9},{11,1... | collective-permute-start | bytes 1179656 | tf_op jit(solution)/shard_map/ppermute | solution.py:230
  81.3 2.9 %collective-permute-start.2 = (bf16[4,96,512]{2,1,0:T(8,128)(2,1)}, bf16[4,96,512]{2,1,0:T(8,128)(2,1)S(1)}, u32[]{:S(2)}, u32[]{:S(2)}) collective-permute-start(bf16[4,96,512]{2,1,0:T(8,128)(2,1)} %bitcast.6), channel_id=1, source_target_pairs={{1,0},{2,1},{3,2},{0,3},{5,4},{6,5},{7,6},{4,7},{9,8},{10,9},{11,1... | collective-permute-start | bytes 1179656 | tf_op jit(solution)/shard_map/ppermute | solution.py:232
  84.2 2.4 %collective-permute-start.1 = (bf16[4,96,512]{2,1,0:T(8,128)(2,1)S(1)}, bf16[4,96,512]{2,1,0:T(8,128)(2,1)S(1)}, u32[]{:S(2)}, u32[]{:S(2)}) collective-permute-start(bf16[4,96,512]{2,1,0:T(8,128)(2,1)S(1)} %bitcast.19), channel_id=1, source_target_pairs={{0,1},{1,2},{2,3},{3,0},{4,5},{5,6},{6,7},{7,4},{8,9},{9,10},{10,1... | collective-permute-start | bytes 1179656 | tf_op jit(solution)/shard_map/ppermute | solution.py:231
  86.6 0.0 collective-permute-done.left_low
  86.6 0.0 copy-start.3
  86.6 1.9 collective-permute-start.4
  88.5 0.0 collective-permute-done.3.right_high
  88.6 0.0 copy-start.4
  88.6 4.6 %collective-permute-start.5 = (bf16[4,96,512]{2,1,0:T(8,128)(2,1)S(1)}, bf16[4,96,512]{2,1,0:T(8,128)(2,1)S(1)}, u32[]{:S(2)}, u32[]{:S(2)}) collective-permute-start(bf16[4,96,512]{2,1,0:T(8,128)(2,1)S(1)} %collective-permute-done.3.right_high), channel_id=1, source_target_pairs={{1,0},{2,1},{3,2},{0,3},{5,4},{6,5},{7,6},{4,7},{9,8},{10,9},{11,1... | collective-permute-start | bytes 1179656 | tf_op jit(solution)/shard_map/ppermute | solution.py:234
  93.1 0.0 collective-permute-done.2.right_low
  93.2 0.0 copy-start.5
  93.2 2.8 %collective-permute-done.1.left_high = bf16[4,96,512]{2,1,0:T(8,128)(2,1)S(1)} collective-permute-done((bf16[4,96,512]{2,1,0:T(8,128)(2,1)S(1)}, bf16[4,96,512]{2,1,0:T(8,128)(2,1)S(1)}, u32[]{:S(2)}, u32[]{:S(2)}) %collective-permute-start.1) | collective-permute-done | bytes 393248 | tf_op jit(solution)/shard_map/ppermute | solution.py:231
  96.0 0.0 copy-start.6
  96.0 6.5 %collective-permute-done.4.far_low = bf16[4,96,512]{2,1,0:T(8,128)(2,1)S(1)} collective-permute-done((bf16[4,96,512]{2,1,0:T(8,128)(2,1)S(1)}, bf16[4,96,512]{2,1,0:T(8,128)(2,1)S(1)}, u32[]{:S(2)}, u32[]{:S(2)}) %collective-permute-start.4) | collective-permute-done | bytes 393248 | tf_op jit(solution)/shard_map/ppermute | solution.py:233
  102.5 0.0 copy-start.7
  102.5 0.0 collective-permute-done.5.far_high
  102.5 0.0 copy-start.8
  102.5 3.6 %all-gather.3.cloned.1.call-done.first_ref = bf16[3072,640]{1,0:T(8,128)(2,1)} async-done(((bf16[384,640]{1,0:T(8,128)(2,1)}), bf16[3072,640]{1,0:T(8,128)(2,1)}) %all-gather.3.cloned.1.call-update) | async-done | bytes 3932176 | tf_op jit(solution)/shard_map/all_gather | solution.py:227
  106.1 0.0 copy-done.2
  106.1 0.0 copy-done.3
  106.1 0.0 copy-done.4
  106.1 0.0 copy-done.5
  106.1 0.0 copy-done.6
  106.1 0.0 copy-done.7
  106.2 0.0 copy-done.8
  106.2 11.6 %shard_map.88 = (bf16[4,8,96,512]{3,2,1,0:T(8,128)(2,1)}, bf16[8,384,640]{2,1,0:T(8,128)(2,1)}) custom-call(s32[1]{0:T(128)} %bitcast.2.x_index, bf16[3072,640]{1,0:T(8,128)(2,1)} %all-gather.3.cloned.1.call-done.first_ref, bf16[8,96,512]{2,1,0:T(8,128)(2,1)} %bitcast.16, bf16[4,96,512]{2,1,0:T(8,128)(2,1)} %copy-done.3, bf16[4,96,512]{2,1,0:T(8,128)(2,1)} %copy-done.6, ...), custom_call_target="tpu_custom_call" | custom-call | tf_op jit(solution)/shard_map/pallas_call | solution.py:204
  117.7 0.0 reduce-scatter.2.cloned.1.call-update
  117.8 37.6 %all_to_all.26 = bf16[4,8,96,512]{3,2,1,0:T(8,128)(2,1)S(1)} all-to-all(bf16[4,8,96,512]{3,2,1,0:T(8,128)(2,1)} %get-tuple-element.16), channel_id=1, replica_groups=mesh['y'=8,'c'=2,'z'=8,'x'=4] {'x'}, dimensions={0} | all-to-all | bytes 6291456 | tf_op jit(solution)/shard_map/all_to_all | solution.py:261
  155.3 1.6 reduce_sum.12
  156.9 0.0 copy-start
  156.9 29.3 %all_to_all.27.first_ref = bf16[8,96,512]{2,1,0:T(8,128)(2,1)S(1)} all-to-all(bf16[8,96,512]{2,1,0:T(8,128)(2,1)} %reduce_sum.12), channel_id=1, replica_groups=mesh['y'=8,'c'=2,'z'=8,'x'=4] {'z'}, dimensions={0} | all-to-all | bytes 1572864 | tf_op jit(solution)/shard_map/all_to_all | solution.py:263
  186.3 11.0 %all_to_all.28.second_ref = bf16[4,96,640]{2,1,0:T(8,128)(2,1)S(1)} all-to-all(bf16[4,96,640]{2,1,0:T(8,128)(2,1)} %bitcast.17), channel_id=1, replica_groups=mesh['y'=8,'c'=2,'z'=8,'x'=4] {'x'}, dimensions={0} | all-to-all | bytes 983040 | tf_op jit(solution)/shard_map/all_to_all | solution.py:265
  197.3 1.6 shard_map.89
  198.9 24.7 %all_to_all.29.rows_ref = bf16[16,36,192]{2,1,0:T(8,128)(2,1)S(1)} all-to-all(bf16[16,36,192]{2,1,0:T(8,128)(2,1)S(1)} %shard_map.89), channel_id=1, replica_groups=mesh['y'=8,'c'=2,'z'=8,'x'=4] {'y','c'}, dimensions={0} | all-to-all | bytes 442368 | tf_op jit(solution)/shard_map/all_to_all | solution.py:268
  223.6 0.0 copy-done
  223.6 0.0 copy-done.1
  223.6 1.5 shard_map.90
  (2 shorter events, 0.0 us)
Async XLA Ops:
  7.2 99.0 %all-gather.3.cloned.1.call-start = ((), (), s32[]{:S(2)}) async-start(), calls=%async_computation.6 | async-start | bytes 4423680 | tf_op jit(solution)/shard_map/all_gather | solution.py:227
  46.0 140.2 %reduce-scatter.2.cloned.1.call-start = ((), (), s32[]{:S(2)}) async-start(), calls=%async_computation.7 | async-start | bytes 4423680 | tf_op jit(solution)/shard_map/reduce_scatter | solution.py:260
  73.9 32.2 %copy-start.2 = (bf16[768,512]{1,0:T(8,128)(2,1)}, bf16[768,512]{1,0:T(8,128)(2,1)S(1)}, u32[]{:S(2)}) copy-start(bf16[768,512]{1,0:T(8,128)(2,1)S(1)} %all-gather) | copy-start | bytes 2359300
  74.8 11.8 %collective-permute-start = (bf16[4,96,512]{2,1,0:T(8,128)(2,1)}, bf16[4,96,512]{2,1,0:T(8,128)(2,1)S(1)}, u32[]{:S(2)}, u32[]{:S(2)}) collective-permute-start(bf16[4,96,512]{2,1,0:T(8,128)(2,1)} %bitcast.6), channel_id=1, source_target_pairs={{0,1},{1,2},{2,3},{3,0},{4,5},{5,6},{6,7},{7,4},{8,9},{9,10},{10,1... | collective-permute-start | bytes 1179656 | tf_op jit(solution)/shard_map/ppermute | solution.py:229
  77.7 10.8 %collective-permute-start.3 = (bf16[4,96,512]{2,1,0:T(8,128)(2,1)S(1)}, bf16[4,96,512]{2,1,0:T(8,128)(2,1)S(1)}, u32[]{:S(2)}, u32[]{:S(2)}) collective-permute-start(bf16[4,96,512]{2,1,0:T(8,128)(2,1)S(1)} %bitcast.18), channel_id=1, source_target_pairs={{1,0},{2,1},{3,2},{0,3},{5,4},{6,5},{7,6},{4,7},{9,8},{10,9},{11,1... | collective-permute-start | bytes 1179656 | tf_op jit(solution)/shard_map/ppermute | solution.py:230
  81.3 11.9 %collective-permute-start.2 = (bf16[4,96,512]{2,1,0:T(8,128)(2,1)}, bf16[4,96,512]{2,1,0:T(8,128)(2,1)S(1)}, u32[]{:S(2)}, u32[]{:S(2)}) collective-permute-start(bf16[4,96,512]{2,1,0:T(8,128)(2,1)} %bitcast.6), channel_id=1, source_target_pairs={{1,0},{2,1},{3,2},{0,3},{5,4},{6,5},{7,6},{4,7},{9,8},{10,9},{11,1... | collective-permute-start | bytes 1179656 | tf_op jit(solution)/shard_map/ppermute | solution.py:232
  84.2 11.8 %collective-permute-start.1 = (bf16[4,96,512]{2,1,0:T(8,128)(2,1)S(1)}, bf16[4,96,512]{2,1,0:T(8,128)(2,1)S(1)}, u32[]{:S(2)}, u32[]{:S(2)}) collective-permute-start(bf16[4,96,512]{2,1,0:T(8,128)(2,1)S(1)} %bitcast.19), channel_id=1, source_target_pairs={{0,1},{1,2},{2,3},{3,0},{4,5},{5,6},{6,7},{7,4},{8,9},{9,10},{10,1... | collective-permute-start | bytes 1179656 | tf_op jit(solution)/shard_map/ppermute | solution.py:231
  86.6 19.5 %copy-start.3 = (bf16[4,96,512]{2,1,0:T(8,128)(2,1)}, bf16[4,96,512]{2,1,0:T(8,128)(2,1)S(1)}, u32[]{:S(2)}) copy-start(bf16[4,96,512]{2,1,0:T(8,128)(2,1)S(1)} %collective-permute-done.left_low) | copy-start | bytes 1179652
  86.6 15.9 %collective-permute-start.4 = (bf16[4,96,512]{2,1,0:T(8,128)(2,1)S(1)}, bf16[4,96,512]{2,1,0:T(8,128)(2,1)S(1)}, u32[]{:S(2)}, u32[]{:S(2)}) collective-permute-start(bf16[4,96,512]{2,1,0:T(8,128)(2,1)S(1)} %collective-permute-done.left_low), channel_id=1, source_target_pairs={{0,1},{1,2},{2,3},{3,0},{4,5},{5,6},{6,7},{7,4},{8,9},{9,10},{10,1... | collective-permute-start | bytes 1179656 | tf_op jit(solution)/shard_map/ppermute | solution.py:233
  88.6 17.6 %copy-start.4 = (bf16[4,96,512]{2,1,0:T(8,128)(2,1)}, bf16[4,96,512]{2,1,0:T(8,128)(2,1)S(1)}, u32[]{:S(2)}) copy-start(bf16[4,96,512]{2,1,0:T(8,128)(2,1)S(1)} %collective-permute-done.3.right_high) | copy-start | bytes 1179652
  88.6 14.0 %collective-permute-start.5 = (bf16[4,96,512]{2,1,0:T(8,128)(2,1)S(1)}, bf16[4,96,512]{2,1,0:T(8,128)(2,1)S(1)}, u32[]{:S(2)}, u32[]{:S(2)}) collective-permute-start(bf16[4,96,512]{2,1,0:T(8,128)(2,1)S(1)} %collective-permute-done.3.right_high), channel_id=1, source_target_pairs={{1,0},{2,1},{3,2},{0,3},{5,4},{6,5},{7,6},{4,7},{9,8},{10,9},{11,1... | collective-permute-start | bytes 1179656 | tf_op jit(solution)/shard_map/ppermute | solution.py:234
  93.2 13.0 %copy-start.5 = (bf16[4,96,512]{2,1,0:T(8,128)(2,1)}, bf16[4,96,512]{2,1,0:T(8,128)(2,1)S(1)}, u32[]{:S(2)}) copy-start(bf16[4,96,512]{2,1,0:T(8,128)(2,1)S(1)} %collective-permute-done.2.right_low) | copy-start | bytes 1179652
  96.0 10.1 %copy-start.6 = (bf16[4,96,512]{2,1,0:T(8,128)(2,1)}, bf16[4,96,512]{2,1,0:T(8,128)(2,1)S(1)}, u32[]{:S(2)}) copy-start(bf16[4,96,512]{2,1,0:T(8,128)(2,1)S(1)} %collective-permute-done.1.left_high) | copy-start | bytes 1179652
  102.5 3.6 %copy-start.7 = (bf16[4,96,512]{2,1,0:T(8,128)(2,1)}, bf16[4,96,512]{2,1,0:T(8,128)(2,1)S(1)}, u32[]{:S(2)}) copy-start(bf16[4,96,512]{2,1,0:T(8,128)(2,1)S(1)} %collective-permute-done.4.far_low) | copy-start | bytes 1179652
  102.5 3.6 %copy-start.8 = (bf16[4,96,512]{2,1,0:T(8,128)(2,1)}, bf16[4,96,512]{2,1,0:T(8,128)(2,1)S(1)}, u32[]{:S(2)}) copy-start(bf16[4,96,512]{2,1,0:T(8,128)(2,1)S(1)} %collective-permute-done.5.far_high) | copy-start | bytes 1179652
  156.9 66.6 %copy-start = (s32[128,4]{0,1:T(4,128)S(1)}, s32[128,4]{0,1:T(4,128)}, u32[]{:S(2)}) copy-start(s32[128,4]{0,1:T(4,128)} %param.8) | copy-start | bytes 6148
  156.9 66.6 %copy-start.1 = (s32[128,4]{0,1:T(4,128)S(1)}, s32[128,4]{0,1:T(4,128)}, u32[]{:S(2)}) copy-start(s32[128,4]{0,1:T(4,128)} %param.9) | copy-start | bytes 6148
Sparse Core Ops, SparseCore 0:
  46.2 59.9 all-gather.2
  117.9 63.0 reduce-scatter.1

commit v5 on v4

--- a/solution.py
+++ b/solution.py
@@ -169,8 +169,9 @@
     for number, (source, planes, away) in enumerate(pieces):
         target = second.at[planes, lax.rem(me + away, 4)]
         loads.append(pltpu.make_async_copy(source, target, sems.at[4 + number]))
-    start_all(loads)
+    start_all(loads[:3])
     wait_all(loads[:2])
+    start_all(loads[3:])
     pre_gate = f32_dot(gate[0], first[...], NN)
     loads[2].wait()
     pre_up = f32_dot(up[0], first[...], NN)

time: 233 us -> 233 us (level)
  no operation moved by 1% of the time
where the time goes in v5:
time: 233 us; the launch traced here: 232 us
  blocking collectives  166 us (71%)
  starting transfers between devices  18.3 us (8%)
  Pallas kernels  17.9 us (8%)
  between operations  14.2 us (6%)
  waiting for transfers between devices  13 us (6%)
    all_to_all x1, blocking collectives, shards(): y_first = lax.all_to_all(y_first, 'x', 0, 0, tiled=True)  37.6 us
    all_to_all x1, blocking collectives, shards(): y_first = lax.all_to_all(y_first, 'z', 0, 0, tiled=True)  29.3 us
    all_gather x1, blocking collectives, shards(): own = lax.all_gather(second, 'z', axis=0, tiled=False)  27.8 us
    all_to_all x1, blocking collectives, shards(): home = lax.all_to_all(back, EP, 0, 0, tiled=True)  24.7 us
    all_to_all x1, blocking collectives, shards(): received = lax.all_to_all(send, EP, 0, 0, tiled=True)  23.2 us
    pallas_call x5, Pallas kernels, call(): pl.pallas_call(body, out_shape=outs, in_specs=specs or [vmem] * len(args)...  17.9 us
    all_gather x1, blocking collectives, shards(): first = lax.all_gather(first, 'x', axis=0, tiled=True)  12.3 us
    all_to_all x1, blocking collectives, shards(): lax.all_to_all(y_second.reshape(4, FEATURES, WIDE), 'x', 0, 0, tiled=True)  11 us
  transfers between devices with their start and end apart: 8, of which 3 were waited for; matrix products, arithmetic and copies ran while one was open for 1% of the time, Pallas kernels for 0%

profile of v5, /device:TPU:1, one launch (start us, length us, event | category | flops | bytes accessed | tf_op | source)
XLA Modules:
  0.0 231.9 jit_solution(7596618887989678494)
XLA Ops:
  7.2 0.0 all-gather.3.cloned.1.call-start
  7.2 2.2 shard_map.86
  9.4 23.2 %all_to_all.25.rows_ref = bf16[16,36,192]{2,1,0:T(8,128)(2,1)S(1)} all-to-all(bf16[16,36,192]{2,1,0:T(8,128)(2,1)} %shard_map.86), channel_id=1, replica_groups=mesh['y'=8,'c'=2,'z'=8,'x'=4] {'y','c'}, dimensions={0} | all-to-all | bytes 442368 | tf_op jit(solution)/shard_map/all_to_all | solution.py:223
  32.7 1.0 shard_map.87
  33.7 12.3 %all_gather.12 = bf16[384,640]{1,0:T(8,128)(2,1)} all-gather(bf16[96,640]{1,0:T(8,128)(2,1)S(1)} %get-tuple-element.12), channel_id=1, replica_groups=mesh['y'=8,'c'=2,'z'=8,'x'=4] {'x'}, dimensions={0}, use_global_device_ids=true | all-gather | bytes 614400 | tf_op jit(solution)/shard_map/all_gather | solution.py:226
  46.0 0.0 all-gather.3.cloned.1.call-update
  46.0 0.0 reduce-scatter.2.cloned.1.call-start
  46.1 27.8 %all-gather = bf16[768,512]{1,0:T(8,128)(2,1)S(1)} all-gather(bf16[96,512]{1,0:T(8,128)(2,1)S(1)} %get-tuple-element.15), channel_id=2, replica_groups=mesh['y'=8,'c'=2,'z'=8,'x'=4] {'z'}, dimensions={0}, use_global_device_ids=true | all-gather | bytes 884736 | tf_op jit(solution)/shard_map/all_gather | solution.py:229
  73.9 0.0 copy-start.2
  73.9 0.9 fusion
  74.8 2.9 %collective-permute-start = (bf16[4,96,512]{2,1,0:T(8,128)(2,1)}, bf16[4,96,512]{2,1,0:T(8,128)(2,1)S(1)}, u32[]{:S(2)}, u32[]{:S(2)}) collective-permute-start(bf16[4,96,512]{2,1,0:T(8,128)(2,1)} %bitcast.6), channel_id=1, source_target_pairs={{0,1},{1,2},{2,3},{3,0},{4,5},{5,6},{6,7},{7,4},{8,9},{9,10},{10,1... | collective-permute-start | bytes 1179656 | tf_op jit(solution)/shard_map/ppermute | solution.py:230
  77.7 3.6 %collective-permute-start.3 = (bf16[4,96,512]{2,1,0:T(8,128)(2,1)S(1)}, bf16[4,96,512]{2,1,0:T(8,128)(2,1)S(1)}, u32[]{:S(2)}, u32[]{:S(2)}) collective-permute-start(bf16[4,96,512]{2,1,0:T(8,128)(2,1)S(1)} %bitcast.18), channel_id=1, source_target_pairs={{1,0},{2,1},{3,2},{0,3},{5,4},{6,5},{7,6},{4,7},{9,8},{10,9},{11,1... | collective-permute-start | bytes 1179656 | tf_op jit(solution)/shard_map/ppermute | solution.py:231
  81.3 2.9 %collective-permute-start.2 = (bf16[4,96,512]{2,1,0:T(8,128)(2,1)}, bf16[4,96,512]{2,1,0:T(8,128)(2,1)S(1)}, u32[]{:S(2)}, u32[]{:S(2)}) collective-permute-start(bf16[4,96,512]{2,1,0:T(8,128)(2,1)} %bitcast.6), channel_id=1, source_target_pairs={{1,0},{2,1},{3,2},{0,3},{5,4},{6,5},{7,6},{4,7},{9,8},{10,9},{11,1... | collective-permute-start | bytes 1179656 | tf_op jit(solution)/shard_map/ppermute | solution.py:233
  84.2 2.4 %collective-permute-start.1 = (bf16[4,96,512]{2,1,0:T(8,128)(2,1)S(1)}, bf16[4,96,512]{2,1,0:T(8,128)(2,1)S(1)}, u32[]{:S(2)}, u32[]{:S(2)}) collective-permute-start(bf16[4,96,512]{2,1,0:T(8,128)(2,1)S(1)} %bitcast.19), channel_id=1, source_target_pairs={{0,1},{1,2},{2,3},{3,0},{4,5},{5,6},{6,7},{7,4},{8,9},{9,10},{10,1... | collective-permute-start | bytes 1179656 | tf_op jit(solution)/shard_map/ppermute | solution.py:232
  86.6 0.0 collective-permute-done.left_low
  86.6 0.0 copy-start.3
  86.6 1.9 collective-permute-start.4
  88.5 0.0 collective-permute-done.3.right_high
  88.6 0.0 copy-start.4
  88.6 4.6 %collective-permute-start.5 = (bf16[4,96,512]{2,1,0:T(8,128)(2,1)S(1)}, bf16[4,96,512]{2,1,0:T(8,128)(2,1)S(1)}, u32[]{:S(2)}, u32[]{:S(2)}) collective-permute-start(bf16[4,96,512]{2,1,0:T(8,128)(2,1)S(1)} %collective-permute-done.3.right_high), channel_id=1, source_target_pairs={{1,0},{2,1},{3,2},{0,3},{5,4},{6,5},{7,6},{4,7},{9,8},{10,9},{11,1... | collective-permute-start | bytes 1179656 | tf_op jit(solution)/shard_map/ppermute | solution.py:235
  93.1 0.0 collective-permute-done.2.right_low
  93.2 0.0 copy-start.5
  93.2 2.8 %collective-permute-done.1.left_high = bf16[4,96,512]{2,1,0:T(8,128)(2,1)S(1)} collective-permute-done((bf16[4,96,512]{2,1,0:T(8,128)(2,1)S(1)}, bf16[4,96,512]{2,1,0:T(8,128)(2,1)S(1)}, u32[]{:S(2)}, u32[]{:S(2)}) %collective-permute-start.1) | collective-permute-done | bytes 393248 | tf_op jit(solution)/shard_map/ppermute | solution.py:232
  96.0 0.0 copy-start.6
  96.0 6.5 %collective-permute-done.4.far_low = bf16[4,96,512]{2,1,0:T(8,128)(2,1)S(1)} collective-permute-done((bf16[4,96,512]{2,1,0:T(8,128)(2,1)S(1)}, bf16[4,96,512]{2,1,0:T(8,128)(2,1)S(1)}, u32[]{:S(2)}, u32[]{:S(2)}) %collective-permute-start.4) | collective-permute-done | bytes 393248 | tf_op jit(solution)/shard_map/ppermute | solution.py:234
  102.5 0.0 copy-start.7
  102.5 0.0 collective-permute-done.5.far_high
  102.5 0.0 copy-start.8
  102.5 3.6 %all-gather.3.cloned.1.call-done.first_ref = bf16[3072,640]{1,0:T(8,128)(2,1)} async-done(((bf16[384,640]{1,0:T(8,128)(2,1)}), bf16[3072,640]{1,0:T(8,128)(2,1)}) %all-gather.3.cloned.1.call-update) | async-done | bytes 3932176 | tf_op jit(solution)/shard_map/all_gather | solution.py:228
  106.1 0.0 copy-done.2
  106.1 0.0 copy-done.3
  106.1 0.0 copy-done.4
  106.1 0.0 copy-done.5
  106.1 0.0 copy-done.6
  106.1 0.0 copy-done.7
  106.2 0.0 copy-done.8
  106.2 11.6 %shard_map.88 = (bf16[4,8,96,512]{3,2,1,0:T(8,128)(2,1)}, bf16[8,384,640]{2,1,0:T(8,128)(2,1)}) custom-call(s32[1]{0:T(128)} %bitcast.2.x_index, bf16[3072,640]{1,0:T(8,128)(2,1)} %all-gather.3.cloned.1.call-done.first_ref, bf16[8,96,512]{2,1,0:T(8,128)(2,1)} %bitcast.16, bf16[4,96,512]{2,1,0:T(8,128)(2,1)} %copy-done.3, bf16[4,96,512]{2,1,0:T(8,128)(2,1)} %copy-done.6, ...), custom_call_target="tpu_custom_call" | custom-call | tf_op jit(solution)/shard_map/pallas_call | solution.py:205
  117.7 0.0 reduce-scatter.2.cloned.1.call-update
  117.8 37.6 %all_to_all.26 = bf16[4,8,96,512]{3,2,1,0:T(8,128)(2,1)S(1)} all-to-all(bf16[4,8,96,512]{3,2,1,0:T(8,128)(2,1)} %get-tuple-element.16), channel_id=1, replica_groups=mesh['y'=8,'c'=2,'z'=8,'x'=4] {'x'}, dimensions={0} | all-to-all | bytes 6291456 | tf_op jit(solution)/shard_map/all_to_all | solution.py:262
  155.3 1.6 reduce_sum.12
  156.9 0.0 copy-start
  156.9 29.3 %all_to_all.27.first_ref = bf16[8,96,512]{2,1,0:T(8,128)(2,1)S(1)} all-to-all(bf16[8,96,512]{2,1,0:T(8,128)(2,1)} %reduce_sum.12), channel_id=1, replica_groups=mesh['y'=8,'c'=2,'z'=8,'x'=4] {'z'}, dimensions={0} | all-to-all | bytes 1572864 | tf_op jit(solution)/shard_map/all_to_all | solution.py:264
  186.3 11.0 %all_to_all.28.second_ref = bf16[4,96,640]{2,1,0:T(8,128)(2,1)S(1)} all-to-all(bf16[4,96,640]{2,1,0:T(8,128)(2,1)} %bitcast.17), channel_id=1, replica_groups=mesh['y'=8,'c'=2,'z'=8,'x'=4] {'x'}, dimensions={0} | all-to-all | bytes 983040 | tf_op jit(solution)/shard_map/all_to_all | solution.py:266
  197.3 1.6 shard_map.89
  198.9 24.7 %all_to_all.29.rows_ref = bf16[16,36,192]{2,1,0:T(8,128)(2,1)S(1)} all-to-all(bf16[16,36,192]{2,1,0:T(8,128)(2,1)S(1)} %shard_map.89), channel_id=1, replica_groups=mesh['y'=8,'c'=2,'z'=8,'x'=4] {'y','c'}, dimensions={0} | all-to-all | bytes 442368 | tf_op jit(solution)/shard_map/all_to_all | solution.py:269
  223.6 0.0 copy-done
  223.6 0.0 copy-done.1
  223.6 1.5 shard_map.90
  (2 shorter events, 0.0 us)
Async XLA Ops:
  7.2 99.0 %all-gather.3.cloned.1.call-start = ((), (), s32[]{:S(2)}) async-start(), calls=%async_computation.6 | async-start | bytes 4423680 | tf_op jit(solution)/shard_map/all_gather | solution.py:228
  46.0 140.2 %reduce-scatter.2.cloned.1.call-start = ((), (), s32[]{:S(2)}) async-start(), calls=%async_computation.7 | async-start | bytes 4423680 | tf_op jit(solution)/shard_map/reduce_scatter | solution.py:261
  73.9 32.2 %copy-start.2 = (bf16[768,512]{1,0:T(8,128)(2,1)}, bf16[768,512]{1,0:T(8,128)(2,1)S(1)}, u32[]{:S(2)}) copy-start(bf16[768,512]{1,0:T(8,128)(2,1)S(1)} %all-gather) | copy-start | bytes 2359300
  74.8 11.8 %collective-permute-start = (bf16[4,96,512]{2,1,0:T(8,128)(2,1)}, bf16[4,96,512]{2,1,0:T(8,128)(2,1)S(1)}, u32[]{:S(2)}, u32[]{:S(2)}) collective-permute-start(bf16[4,96,512]{2,1,0:T(8,128)(2,1)} %bitcast.6), channel_id=1, source_target_pairs={{0,1},{1,2},{2,3},{3,0},{4,5},{5,6},{6,7},{7,4},{8,9},{9,10},{10,1... | collective-permute-start | bytes 1179656 | tf_op jit(solution)/shard_map/ppermute | solution.py:230
  77.7 10.8 %collective-permute-start.3 = (bf16[4,96,512]{2,1,0:T(8,128)(2,1)S(1)}, bf16[4,96,512]{2,1,0:T(8,128)(2,1)S(1)}, u32[]{:S(2)}, u32[]{:S(2)}) collective-permute-start(bf16[4,96,512]{2,1,0:T(8,128)(2,1)S(1)} %bitcast.18), channel_id=1, source_target_pairs={{1,0},{2,1},{3,2},{0,3},{5,4},{6,5},{7,6},{4,7},{9,8},{10,9},{11,1... | collective-permute-start | bytes 1179656 | tf_op jit(solution)/shard_map/ppermute | solution.py:231
  81.3 11.9 %collective-permute-start.2 = (bf16[4,96,512]{2,1,0:T(8,128)(2,1)}, bf16[4,96,512]{2,1,0:T(8,128)(2,1)S(1)}, u32[]{:S(2)}, u32[]{:S(2)}) collective-permute-start(bf16[4,96,512]{2,1,0:T(8,128)(2,1)} %bitcast.6), channel_id=1, source_target_pairs={{1,0},{2,1},{3,2},{0,3},{5,4},{6,5},{7,6},{4,7},{9,8},{10,9},{11,1... | collective-permute-start | bytes 1179656 | tf_op jit(solution)/shard_map/ppermute | solution.py:233
  84.2 11.8 %collective-permute-start.1 = (bf16[4,96,512]{2,1,0:T(8,128)(2,1)S(1)}, bf16[4,96,512]{2,1,0:T(8,128)(2,1)S(1)}, u32[]{:S(2)}, u32[]{:S(2)}) collective-permute-start(bf16[4,96,512]{2,1,0:T(8,128)(2,1)S(1)} %bitcast.19), channel_id=1, source_target_pairs={{0,1},{1,2},{2,3},{3,0},{4,5},{5,6},{6,7},{7,4},{8,9},{9,10},{10,1... | collective-permute-start | bytes 1179656 | tf_op jit(solution)/shard_map/ppermute | solution.py:232
  86.6 19.5 %copy-start.3 = (bf16[4,96,512]{2,1,0:T(8,128)(2,1)}, bf16[4,96,512]{2,1,0:T(8,128)(2,1)S(1)}, u32[]{:S(2)}) copy-start(bf16[4,96,512]{2,1,0:T(8,128)(2,1)S(1)} %collective-permute-done.left_low) | copy-start | bytes 1179652
  86.6 15.9 %collective-permute-start.4 = (bf16[4,96,512]{2,1,0:T(8,128)(2,1)S(1)}, bf16[4,96,512]{2,1,0:T(8,128)(2,1)S(1)}, u32[]{:S(2)}, u32[]{:S(2)}) collective-permute-start(bf16[4,96,512]{2,1,0:T(8,128)(2,1)S(1)} %collective-permute-done.left_low), channel_id=1, source_target_pairs={{0,1},{1,2},{2,3},{3,0},{4,5},{5,6},{6,7},{7,4},{8,9},{9,10},{10,1... | collective-permute-start | bytes 1179656 | tf_op jit(solution)/shard_map/ppermute | solution.py:234
  88.6 17.6 %copy-start.4 = (bf16[4,96,512]{2,1,0:T(8,128)(2,1)}, bf16[4,96,512]{2,1,0:T(8,128)(2,1)S(1)}, u32[]{:S(2)}) copy-start(bf16[4,96,512]{2,1,0:T(8,128)(2,1)S(1)} %collective-permute-done.3.right_high) | copy-start | bytes 1179652
  88.6 14.0 %collective-permute-start.5 = (bf16[4,96,512]{2,1,0:T(8,128)(2,1)S(1)}, bf16[4,96,512]{2,1,0:T(8,128)(2,1)S(1)}, u32[]{:S(2)}, u32[]{:S(2)}) collective-permute-start(bf16[4,96,512]{2,1,0:T(8,128)(2,1)S(1)} %collective-permute-done.3.right_high), channel_id=1, source_target_pairs={{1,0},{2,1},{3,2},{0,3},{5,4},{6,5},{7,6},{4,7},{9,8},{10,9},{11,1... | collective-permute-start | bytes 1179656 | tf_op jit(solution)/shard_map/ppermute | solution.py:235
  93.2 13.0 %copy-start.5 = (bf16[4,96,512]{2,1,0:T(8,128)(2,1)}, bf16[4,96,512]{2,1,0:T(8,128)(2,1)S(1)}, u32[]{:S(2)}) copy-start(bf16[4,96,512]{2,1,0:T(8,128)(2,1)S(1)} %collective-permute-done.2.right_low) | copy-start | bytes 1179652
  96.0 10.1 %copy-start.6 = (bf16[4,96,512]{2,1,0:T(8,128)(2,1)}, bf16[4,96,512]{2,1,0:T(8,128)(2,1)S(1)}, u32[]{:S(2)}) copy-start(bf16[4,96,512]{2,1,0:T(8,128)(2,1)S(1)} %collective-permute-done.1.left_high) | copy-start | bytes 1179652
  102.5 3.6 %copy-start.7 = (bf16[4,96,512]{2,1,0:T(8,128)(2,1)}, bf16[4,96,512]{2,1,0:T(8,128)(2,1)S(1)}, u32[]{:S(2)}) copy-start(bf16[4,96,512]{2,1,0:T(8,128)(2,1)S(1)} %collective-permute-done.4.far_low) | copy-start | bytes 1179652
  102.5 3.6 %copy-start.8 = (bf16[4,96,512]{2,1,0:T(8,128)(2,1)}, bf16[4,96,512]{2,1,0:T(8,128)(2,1)S(1)}, u32[]{:S(2)}) copy-start(bf16[4,96,512]{2,1,0:T(8,128)(2,1)S(1)} %collective-permute-done.5.far_high) | copy-start | bytes 1179652
  156.9 66.6 %copy-start = (s32[128,4]{0,1:T(4,128)S(1)}, s32[128,4]{0,1:T(4,128)}, u32[]{:S(2)}) copy-start(s32[128,4]{0,1:T(4,128)} %param.8) | copy-start | bytes 6148
  156.9 66.6 %copy-start.1 = (s32[128,4]{0,1:T(4,128)S(1)}, s32[128,4]{0,1:T(4,128)}, u32[]{:S(2)}) copy-start(s32[128,4]{0,1:T(4,128)} %param.9) | copy-start | bytes 6148
Sparse Core Ops, SparseCore 0:
  46.2 59.9 all-gather.2
  117.9 62.9 reduce-scatter.1
